TPU v7x, 512 devices: a whole 4x8x8 slice. The times are simulated.
512 devices in a mesh: dp: 64 (over y, z_hi, core), space: 8 (over z_lo, x).
Axes of the slice: x: 4, y: 8, z: 8 (z_hi: 4, z_lo: 2; z = z_hi * 2 + z_lo), core: 2. Of those that a mesh axis runs over, the one named last changes fastest.
Arguments:
- expanded: bfloat16 [512, 32, 16, 1152], P('dp', 'space'), may hold values from -6 to 6
- dw_four: float32 [9, 1152], replicated, may hold values from -2 to 2
- squeeze_down: bfloat16 [1152, 86], replicated, may hold values from -0.75 to 0.75
- squeeze_up: bfloat16 [86, 1152], replicated, may hold values from -1.25 to 1.25
- project_four: bfloat16 [1152, 344], replicated, may hold values from -0.1875 to 0.1875
- expand_five: bfloat16 [344, 1152], replicated, may hold values from -0.3125 to 0.3125
- dw_five: float32 [25, 1152], replicated, may hold values from -1.25 to 1.25
- project_five: bfloat16 [1152, 480], replicated, may hold values from -0.1875 to 0.1875
- cotangent: bfloat16 [512, 32, 16, 480], P(('dp', 'space')), may hold values from -6 to 6
Outputs:
- grad_expand: float32 [344, 1152], P(None, 'dp')
- grad_depthwise: float32 [25, 1152], P(None, 'dp')
- grad_project: float32 [1152, 480], P('dp')
- input_cotangent: bfloat16 [512, 32, 16, 344], P('dp', 'space')
All inputs are finite; a program needn't handle non-finite values.
Results may differ from a plain program's by a relative error of at most 0.018.
Values may be sent and summed in bfloat16 or wider, within the bound.
A program may use at most 64 MiB of HBM per device.

v0:
```python
import math

import jax
import jax.numpy as jnp
from jax import lax
from jax.sharding import PartitionSpec as P


def padded_2(block, sides, width):
    for axis, dim in sides:
        count = lax.axis_size(axis)
        forward = [(i, i + 1) for i in range(count - 1)]
        backward = [(target, source) for source, target in forward]
        low = lax.ppermute(
            lax.slice_in_dim(block, block.shape[dim] - width, None, axis=dim), axis, forward
        )
        high = lax.ppermute(lax.slice_in_dim(block, 0, width, axis=dim), axis, backward)
        block = jnp.concatenate([low, block, high], axis=dim)
    return block


def swish_act(value):
    return value * jax.nn.sigmoid(value)


def swish_slope(value):
    sig_value = jax.nn.sigmoid(value)
    return sig_value * (1.0 + value * (1.0 - sig_value))


def depthwise(padded, kernel, span_cells):
    reach_cells = span_cells // 2
    row_count = padded.shape[1] - 2 * reach_cells
    wide_cols = jnp.pad(padded, ((0, 0), (0, 0), (reach_cells, reach_cells), (0, 0)))
    col_count = padded.shape[2]
    summed = jnp.zeros((padded.shape[0], row_count, col_count, padded.shape[3]), jnp.float32)
    for i in range(span_cells):
        for j in range(span_cells):
            window = wide_cols[:, i : i + row_count, j : j + col_count, :].astype(jnp.float32)
            summed = summed + window * kernel[i * span_cells + j]
    return summed


def kernel_grad(padded, grad_field, span_cells):
    reach_cells = span_cells // 2
    row_count = grad_field.shape[1]
    col_count = grad_field.shape[2]
    wide_cols = jnp.pad(padded, ((0, 0), (0, 0), (reach_cells, reach_cells), (0, 0)))
    taps = []
    for i in range(span_cells):
        for j in range(span_cells):
            window = wide_cols[:, i : i + row_count, j : j + col_count, :].astype(jnp.float32)
            taps.append(jnp.sum(window * grad_field, axis=(0, 1, 2)))
    return jnp.stack(taps, axis=0)


def finish_four(mixed, image_mean, squeeze_down, squeeze_up, project_four):
    squeezed = swish_act(
        jnp.dot(image_mean.astype(jnp.bfloat16), squeeze_down, preferred_element_type=jnp.float32)
    ).astype(jnp.bfloat16)
    gate_vals = jax.nn.sigmoid(jnp.dot(squeezed, squeeze_up, preferred_element_type=jnp.float32))
    hidden = (mixed * gate_vals[:, None, None, :]).astype(jnp.bfloat16)
    s, r, w, e = hidden.shape
    return (
        jnp.dot(hidden.reshape(-1, e), project_four, preferred_element_type=jnp.float32)
        .astype(jnp.bfloat16)
        .reshape(s, r, w, -1)
    )


def section_five(inputs, expand_five, dw_five, project_five, cotangent, factor):
    s, h, w, c = inputs.shape
    flat_rows = inputs.reshape(-1, c)
    pre_act = jnp.dot(flat_rows, expand_five, preferred_element_type=jnp.float32)
    chans = pre_act.shape[1]
    spread = swish_act(pre_act).astype(jnp.bfloat16).reshape(s, h, w, chans)
    padded = jnp.pad(spread, ((0, 0), (2, 2), (0, 0), (0, 0)))
    deep_act = depthwise(padded, dw_five, 5)
    hidden = swish_act(deep_act).astype(jnp.bfloat16).reshape(-1, chans)
    cot_rows = cotangent.reshape(-1, cotangent.shape[3])
    grad_project = lax.dot_general(
        hidden, cot_rows, (((0,), (0,)), ((), ())), preferred_element_type=jnp.float32
    )
    back_hidden = lax.dot_general(
        cot_rows, project_five, (((1,), (1,)), ((), ())), preferred_element_type=jnp.float32
    )
    back_deep = back_hidden.reshape(s, h, w, chans) * swish_slope(deep_act)
    grad_depthwise = kernel_grad(padded, back_deep, 5)
    back_padded = jnp.pad(back_deep, ((0, 0), (2, 2), (0, 0), (0, 0)))
    back_spread = depthwise(back_padded, dw_five[::-1], 5)
    back_pre = (back_spread.reshape(-1, chans) * swish_slope(pre_act)).astype(jnp.bfloat16)
    grad_expand = lax.dot_general(
        flat_rows, back_pre, (((0,), (0,)), ((), ())), preferred_element_type=jnp.float32
    )
    back_inputs = lax.dot_general(
        back_pre, expand_five, (((1,), (1,)), ((), ())), preferred_element_type=jnp.float32
    )
    back_inputs = back_inputs.astype(jnp.bfloat16).reshape(s, h, w, c)
    return (grad_expand * factor, grad_depthwise * factor, grad_project * factor, back_inputs)


def local(
    expanded,
    dw_four,
    squeeze_down,
    squeeze_up,
    project_four,
    expand_five,
    dw_five,
    project_five,
    cotangent,
):
    group_size = lax.axis_size("space")
    full_rows = expanded.shape[1] * group_size
    cell_count = full_rows * expanded.shape[2]
    padded = padded_2(expanded, (("space", 1),), 1)
    mixed = swish_act(depthwise(padded, dw_four, 3))
    summed = lax.psum(jnp.sum(mixed, axis=(1, 2)), "space")
    image_mean = summed / cell_count
    row_out = finish_four(mixed, image_mean, squeeze_down, squeeze_up, project_four)
    section_out = lax.all_to_all(row_out, "space", split_axis=0, concat_axis=1, tiled=True)
    total_pixels = (
        cotangent.shape[0] * group_size * lax.axis_size("dp") * full_rows * expanded.shape[2]
    )
    factor = 1.0 / math.sqrt(total_pixels)
    grad_e, grad_d, grad_p, back_inputs = section_five(
        section_out, expand_five, dw_five, project_five, cotangent, factor
    )
    input_cotangent = lax.all_to_all(back_inputs, "space", split_axis=1, concat_axis=0, tiled=True)
    group_e, group_d, group_p = (
        lax.psum(grad_e.astype(jnp.bfloat16), "space").astype(jnp.float32),
        lax.psum(grad_d.astype(jnp.bfloat16), "space").astype(jnp.float32),
        lax.psum(grad_p.astype(jnp.bfloat16), "space").astype(jnp.float32),
    )
    grad_e, grad_d, grad_p = (
        lax.psum_scatter(group_e, "dp", scatter_dimension=1, tiled=True),
        lax.psum_scatter(group_d, "dp", scatter_dimension=1, tiled=True),
        lax.psum_scatter(group_p, "dp", scatter_dimension=0, tiled=True),
    )
    return (grad_e, grad_d, grad_p, input_cotangent)


def solution(mesh):
    in_specs = (
        P("dp", "space", None, None),
        P(),
        P(),
        P(),
        P(),
        P(),
        P(),
        P(),
        P(("dp", "space"), None, None, None),
    )
    out_specs = (P(None, "dp"), P(None, "dp"), P("dp", None), P("dp", "space", None, None))
    return jax.shard_map(local, mesh=mesh, in_specs=in_specs, out_specs=out_specs, check_vma=False)
```

profile of v0, /device:TPU:6, one launch (start us, length us, event | category | flops | bytes accessed | tf_op | source)
XLA Modules:
  0.0 788.5 jit_solution(14164084958567933486)
XLA Ops:
  8.4 4.3 collective-permute-start
  15.9 3.2 collective-permute-done
  19.2 6.0 collective-permute-done.1
  27.4 3.3 fusion.119
  30.7 30.7 %psum.28 = f32[8,1152]{1,0:T(8,128)S(1)} all-reduce(f32[8,1152]{1,0:T(8,128)S(1)} %get-tuple-element.77), channel_id=1, replica_groups=mesh['dp'=64,'space'=8] {'space'}, use_global_device_ids=true, to_apply=%region_1.2 | all-reduce | flops 9216 | bytes 73728 | tf_op jit(solution)/shard_map/psum | solution.py:118
  65.5 6.2 all-to-all-start
  74.0 3.1 all-to-all-done
  77.1 2.3 multiply_convert_fusion.1
  79.5 8.2 %fusion.34 = f32[1,32,16,1152]{3,2,1,0:T(8,128)S(1)} fusion(f32[1152]{0:T(1024)S(1)} %get-tuple-element.62, f32[1152]{0:T(1024)S(1)} %get-tuple-element.63, f32[1152]{0:T(1024)S(1)} %get-tuple-element.40, f32[1152]{0:T(1024)S(1)} %get-tuple-element.41, f32[1152]{0:T(1024)S(1)} %get-tuple-element.42, f32[1152]{0:T(1024)S(1)} %get-tuple-element.43, ...), kind=kLoop, calls=%fused_computation.128 | loop fusion | flops 43646976 | bytes 9789440 | tf_op jit(solution)/shard_map/add | solution.py:40
  89.6 3.7 fusion.57
  96.5 29.3 %fusion.102 = f32[1,32,16,1152]{3,2,1,0:T(8,128)} fusion(f32[1,36,16,1152]{3,2,1,0:T(8,128)} %pad.24, f32[1,32,16,1152]{3,2,1,0:T(8,128)} %copy-done.1, f32[1152]{0:T(1024)S(1)} %get-tuple-element.62, f32[1152]{0:T(1024)S(1)} %get-tuple-element.63, f32[1152]{0:T(1024)S(1)} %get-tuple-element.40, f32[1152]{0:T(1024)S(1)} %get-tuple-element.41, ...), kind=kLoop, calls=%fused_computation.196 | loop fusion | flops 28901376 | bytes 16925184 | tf_op jit(solution)/shard_map/add | solution.py:40
  125.8 3.2 fusion.104
  131.8 8.6 %fusion.59 = (f32[1152]{0:T(1024)S(1)}, f32[1152]{0:T(1024)S(1)}, f32[1152]{0:T(1024)S(1)}, f32[1152]{0:T(1024)S(1)}, f32[1152]{0:T(1024)S(1)}, /*index=5*/f32[1...) fusion(f32[1,32,16,1152]{3,2,1,0:T(8,128)} %copy-done.1, ...), kind=kLoop, calls=%fused_computation.153 | loop fusion | flops 31829760 | bytes 3769344 | tf_op jit(solution)/shard_map/reduce_sum | solution.py:53
  142.4 6.4 all-to-all-start.1
  149.6 79.0 %all-reduce.14.cloned.1.call-done = (bf16[344,1152]{0,1:T(8,128)(2,1)}, bf16[1152,480]{1,0:T(8,128)(2,1)}) async-done(((bf16[344,1152]{0,1:T(8,128)(2,1)}, bf16[1152,480]{1,0:T(8,128)(2,1)}), (bf16[344,1152]{0,1:T(8,128)(2,1)}, bf16[1152,480]{1,0:T(8,128)(2,1)})) %all-reduce.14.cloned.1.call-update) | async-done | bytes 1898512 | tf_op jit(solution)/shard_map/psum | solution.py:131
  230.2 164.5 %fusion = f32[24,480]{1,0:T(8,128)S(1)} fusion(f32[1152,480]{1,0:T(8,128)S(1)} %convert_element_type.235), kind=kCustom, calls=%all-reduce-scatter | all-reduce-scatter fusion | flops 737281 | bytes 2259968
  396.0 34.2 %psum.30 = bf16[25,1152]{1,0:T(8,128)(2,1)S(1)} all-reduce(bf16[25,1152]{1,0:T(8,128)(2,1)} %multiply_convert_fusion.4), channel_id=1, replica_groups=mesh['dp'=64,'space'=8] {'space'}, use_global_device_ids=true, to_apply=%region_29.30 | all-reduce | flops 28800 | bytes 115200 | tf_op jit(solution)/shard_map/psum | solution.py:132
  437.4 303.5 %all-reduce.15 = (f32[344,1152]{0,1:T(8,128)}, f32[25,1152]{1,0:T(8,128)S(1)}) all-reduce(bf16[344,1152]{0,1:T(8,128)(2,1)} %get-tuple-element.75, bf16[25,1152]{1,0:T(8,128)(2,1)S(1)} %psum.30), channel_id=2, replica_groups=mesh['dp'=64,'space'=8] {'dp'}, use_global_device_ids=true, to_apply=%region_3.4.clone | all-reduce | flops 425088 | bytes 2550528
  744.8 5.9 collective-permute-start.8
  750.7 8.6 %collective-permute-start.7 = (f32[24,480]{1,0:T(8,128)S(1)}, f32[24,480]{1,0:T(8,128)S(1)}, u32[]{:S(2)}, u32[]{:S(2)}) collective-permute-start(f32[24,480]{1,0:T(8,128)S(1)} %fusion), channel_id=1, source_target_pairs={{0,48},{8,56},{16,64},{24,72},{32,80},{40,88},{48,96},{56,104},{64... | collective-permute-start | bytes 138248
  762.0 5.8 collective-permute-start.5
  769.2 3.1 collective-permute-start.3
  772.3 3.9 collective-permute-start.2
  777.0 2.2 concatenate.12
  (103 shorter events, 43.3 us)
Async XLA Ops:
  7.2 82.5 %copy-start = (bf16[1152,480]{0,1:T(8,128)(2,1)S(1)}, bf16[1152,480]{0,1:T(8,128)(2,1)}, u32[]{:S(2)}) copy-start(bf16[1152,480]{0,1:T(8,128)(2,1)} %param.16) | copy-start | bytes 3317764
  8.4 19.0 %copy-start.2 = (bf16[8,4,16,1152]{3,2,1,0:T(8,128)(2,1)S(1)}, bf16[8,4,16,1152]{3,2,1,0:T(8,128)(2,1)}, u32[]{:S(2)}) copy-start(bf16[8,4,16,1152]{3,2,1,0:T(8,128)(2,1)} %param.9) | copy-start | bytes 3538948
  8.4 10.8 %collective-permute-start = (bf16[8,1,16,1152]{3,2,1,0:T(8,128)(2,1)S(1)}, bf16[8,1,16,1152]{3,2,1,0:T(8,128)(2,1)S(1)}, u32[]{:S(2)}, u32[]{:S(2)}) collective-permute-start(bf16[8,1,16,1152]{3,2,1,0:T(8,128)(2,1)S(1)} %get-tuple-element.79), channel_id=1, source_target_pairs={{0,1},{1,2},{2,3},{3,4},{4,5},{5,6},{6,7},{8,9},{9,10},{10,11},{11... | collective-permute-start | bytes 884744 | tf_op jit(solution)/shard_map/ppermute | solution.py:14
  12.7 12.5 %collective-permute-start.1 = (bf16[8,1,16,1152]{3,2,1,0:T(8,128)(2,1)S(1)}, bf16[8,1,16,1152]{3,2,1,0:T(8,128)(2,1)S(1)}, u32[]{:S(2)}, u32[]{:S(2)}) collective-permute-start(bf16[8,1,16,1152]{3,2,1,0:T(8,128)(2,1)S(1)} %get-tuple-element.80), channel_id=1, source_target_pairs={{1,0},{2,1},{3,2},{4,3},{5,4},{6,5},{7,6},{9,8},{10,9},{11,10},{12... | collective-permute-start | bytes 884744 | tf_op jit(solution)/shard_map/ppermute | solution.py:17
  63.0 14.1 %copy-start.8 = (bf16[344,1152]{1,0:T(8,128)(2,1)S(1)}, bf16[344,1152]{1,0:T(8,128)(2,1)}, u32[]{:S(2)}) copy-start(bf16[344,1152]{1,0:T(8,128)(2,1)} %param.14) | copy-start | bytes 2377732
  65.5 11.6 %all-to-all-start = ((bf16[8,4,16,344]{3,2,1,0:T(8,128)(2,1)}), bf16[8,4,16,344]{3,2,1,0:T(8,128)(2,1)S(1)}, u32[]{:S(2)}, u32[]{:S(2)}) async-start(bf16[8,4,16,344]{3,2,1,0:T(8,128)(2,1)} %bitcast.1), calls=%async_computation | async-start | bytes 786432 | tf_op jit(solution)/shard_map/all_to_all | solution.py:121
  71.8 156.8 %all-reduce.14.cloned.1.call-start = ((), (), s32[]{:S(2)}) async-start(), calls=%async_computation.2 | async-start | bytes 4128768 | tf_op jit(solution)/shard_map/psum | solution.py:131
  142.4 287.8 %all-to-all-start.1 = ((bf16[1,32,16,344]{3,2,0,1:T(8,128)(2,1)}), bf16[1,32,16,344]{3,2,0,1:T(8,128)(2,1)}, u32[]{:S(2)}, u32[]{:S(2)}) async-start(bf16[1,32,16,344]{3,2,0,1:T(8,128)(2,1)} %bitcast.11), calls=%async_computation.1 | async-start | bytes 786432 | tf_op jit(solution)/shard_map/all_to_all | solution.py:129
  394.7 40.7 %collective-permute-start.17 = (f32[18,480]{1,0:T(8,128)S(1)}, f32[18,480]{1,0:T(8,128)S(1)}, u32[]{:S(2)}, u32[]{:S(2)}) collective-permute-start(f32[18,480]{1,0:T(8,128)S(1)} %slice.467), channel_id=1, source_target_pairs={{0,128},{8,136},{16,144},{24,152},{32,160},{40,168},{48,176},{56,1... | collective-permute-start | bytes 103688
  430.2 310.7 %collective-permute-start.16 = (f32[24,480]{1,0:T(8,128)S(1)}, f32[24,480]{1,0:T(8,128)S(1)}, u32[]{:S(2)}, u32[]{:S(2)}) collective-permute-start(f32[24,480]{1,0:T(8,128)S(1)} %fusion), channel_id=1, source_target_pairs={{0,120},{8,128},{16,136},{24,144},{32,152},{40,160},{48,168},{56,1... | collective-permute-start | bytes 138248
  431.5 310.7 %collective-permute-start.15 = (f32[24,480]{1,0:T(8,128)S(1)}, f32[24,480]{1,0:T(8,128)S(1)}, u32[]{:S(2)}, u32[]{:S(2)}) collective-permute-start(f32[24,480]{1,0:T(8,128)S(1)} %fusion), channel_id=1, source_target_pairs={{0,112},{8,120},{16,128},{24,136},{32,144},{40,152},{48,160},{56,1... | collective-permute-start | bytes 138248
  432.8 310.7 %collective-permute-start.14 = (f32[24,480]{1,0:T(8,128)S(1)}, f32[24,480]{1,0:T(8,128)S(1)}, u32[]{:S(2)}, u32[]{:S(2)}) collective-permute-start(f32[24,480]{1,0:T(8,128)S(1)} %fusion), channel_id=1, source_target_pairs={{0,104},{8,112},{16,120},{24,128},{32,136},{40,144},{48,152},{56,1... | collective-permute-start | bytes 138248
  434.1 310.7 %collective-permute-start.13 = (f32[24,480]{1,0:T(8,128)S(1)}, f32[24,480]{1,0:T(8,128)S(1)}, u32[]{:S(2)}, u32[]{:S(2)}) collective-permute-start(f32[24,480]{1,0:T(8,128)S(1)} %fusion), channel_id=1, source_target_pairs={{0,96},{8,104},{16,112},{24,120},{32,128},{40,136},{48,144},{56,15... | collective-permute-start | bytes 138248
  435.4 315.4 %collective-permute-start.12 = (f32[24,480]{1,0:T(8,128)S(1)}, f32[24,480]{1,0:T(8,128)S(1)}, u32[]{:S(2)}, u32[]{:S(2)}) collective-permute-start(f32[24,480]{1,0:T(8,128)S(1)} %fusion), channel_id=1, source_target_pairs={{0,88},{8,96},{16,104},{24,112},{32,120},{40,128},{48,136},{56,144... | collective-permute-start | bytes 138248
  740.9 19.9 %collective-permute-start.11 = (f32[24,480]{1,0:T(8,128)S(1)}, f32[24,480]{1,0:T(8,128)S(1)}, u32[]{:S(2)}, u32[]{:S(2)}) collective-permute-start(f32[24,480]{1,0:T(8,128)S(1)} %fusion), channel_id=1, source_target_pairs={{0,80},{8,88},{16,96},{24,104},{32,112},{40,120},{48,128},{56,136}... | collective-permute-start | bytes 138248
  742.2 19.9 %collective-permute-start.10 = (f32[24,480]{1,0:T(8,128)S(1)}, f32[24,480]{1,0:T(8,128)S(1)}, u32[]{:S(2)}, u32[]{:S(2)}) collective-permute-start(f32[24,480]{1,0:T(8,128)S(1)} %fusion), channel_id=1, source_target_pairs={{0,72},{8,80},{16,88},{24,96},{32,104},{40,112},{48,120},{56,128},... | collective-permute-start | bytes 138248
  743.5 24.4 %collective-permute-start.9 = (f32[24,480]{1,0:T(8,128)S(1)}, f32[24,480]{1,0:T(8,128)S(1)}, u32[]{:S(2)}, u32[]{:S(2)}) collective-permute-start(f32[24,480]{1,0:T(8,128)S(1)} %fusion), channel_id=1, source_target_pairs={{0,64},{8,72},{16,80},{24,88},{32,96},{40,104},{48,112},{56,120},{... | collective-permute-start | bytes 138248
  744.8 24.4 %collective-permute-start.8 = (f32[24,480]{1,0:T(8,128)S(1)}, f32[24,480]{1,0:T(8,128)S(1)}, u32[]{:S(2)}, u32[]{:S(2)}) collective-permute-start(f32[24,480]{1,0:T(8,128)S(1)} %fusion), channel_id=1, source_target_pairs={{0,56},{8,64},{16,72},{24,80},{32,88},{40,96},{48,104},{56,112},{6... | collective-permute-start | bytes 138248
  750.7 21.6 %collective-permute-start.7 = (f32[24,480]{1,0:T(8,128)S(1)}, f32[24,480]{1,0:T(8,128)S(1)}, u32[]{:S(2)}, u32[]{:S(2)}) collective-permute-start(f32[24,480]{1,0:T(8,128)S(1)} %fusion), channel_id=1, source_target_pairs={{0,48},{8,56},{16,64},{24,72},{32,80},{40,88},{48,96},{56,104},{64... | collective-permute-start | bytes 138248
  760.7 16.2 %collective-permute-start.6 = (f32[24,480]{1,0:T(8,128)S(1)}, f32[24,480]{1,0:T(8,128)S(1)}, u32[]{:S(2)}, u32[]{:S(2)}) collective-permute-start(f32[24,480]{1,0:T(8,128)S(1)} %fusion), channel_id=1, source_target_pairs={{0,40},{8,48},{16,56},{24,64},{32,72},{40,80},{48,88},{56,96},{64,... | collective-permute-start | bytes 138248
  762.0 14.9 %collective-permute-start.5 = (f32[24,480]{1,0:T(8,128)S(1)}, f32[24,480]{1,0:T(8,128)S(1)}, u32[]{:S(2)}, u32[]{:S(2)}) collective-permute-start(f32[24,480]{1,0:T(8,128)S(1)} %fusion), channel_id=1, source_target_pairs={{0,32},{8,40},{16,48},{24,56},{32,64},{40,72},{48,80},{56,88},{64,... | collective-permute-start | bytes 138248
  767.9 9.1 %collective-permute-start.4 = (f32[24,480]{1,0:T(8,128)S(1)}, f32[24,480]{1,0:T(8,128)S(1)}, u32[]{:S(2)}, u32[]{:S(2)}) collective-permute-start(f32[24,480]{1,0:T(8,128)S(1)} %fusion), channel_id=1, source_target_pairs={{0,24},{8,32},{16,40},{24,48},{32,56},{40,64},{48,72},{56,80},{64,... | collective-permute-start | bytes 138248
  769.2 7.8 collective-permute-start.3
  772.3 4.7 collective-permute-start.2
  (8 other events, 49.1 us)
Sparse Core Ops, SparseCore 0:
  131.9 96.6 all-reduce.13
where the time goes:
time: 800 us; the launch traced here: 789 us
  blocking collectives  533 us (67%)
  waiting for transfers between devices  91.5 us (11%)
  starting transfers between devices  61.1 us (8%)
  other arithmetic  57.1 us (7%)
  local copies, waits for them, and re-layouts  17.6 us (2%)
  between operations  16 us (2%)
  matrix products  12.4 us (2%)
    unnamed x2, blocking collectives  468 us
    psum x1, waiting for transfers between devices, local(): lax.psum(grad_e.astype(jnp.bfloat16), 'space').astype(jnp.float32)  79 us
    unnamed x16, starting transfers between devices  42.2 us
    add x2, other arithmetic, depthwise(): summed = summed + window * kernel[i * span_cells + j]  37.4 us
    psum x1, blocking collectives, local(): lax.psum(grad_d.astype(jnp.bfloat16), 'space').astype(jnp.float32)  34.2 us
    psum x1, blocking collectives, local(): summed = lax.psum(jnp.sum(mixed, axis=(1, 2)), 'space')  30.7 us
  transfers between devices with their start and end apart: 21, of which 5 were waited for; matrix products, arithmetic and copies ran while one was open for 23% of the time, Pallas kernels for 0%

commit v1 on v0

--- a/solution.py
+++ b/solution.py
@@ -6,17 +6,15 @@
 from jax.sharding import PartitionSpec as P
 
 
-def padded_2(block, sides, width):
-    for axis, dim in sides:
-        count = lax.axis_size(axis)
-        forward = [(i, i + 1) for i in range(count - 1)]
-        backward = [(target, source) for source, target in forward]
-        low = lax.ppermute(
-            lax.slice_in_dim(block, block.shape[dim] - width, None, axis=dim), axis, forward
-        )
-        high = lax.ppermute(lax.slice_in_dim(block, 0, width, axis=dim), axis, backward)
-        block = jnp.concatenate([low, block, high], axis=dim)
-    return block
+def padded_2(block, axis, dim, width):
+    count = lax.axis_size(axis)
+    forward = [(i, i + 1) for i in range(count - 1)]
+    backward = [(target, source) for source, target in forward]
+    low = lax.ppermute(
+        lax.slice_in_dim(block, block.shape[dim] - width, None, axis=dim), axis, forward
+    )
+    high = lax.ppermute(lax.slice_in_dim(block, 0, width, axis=dim), axis, backward)
+    return jnp.concatenate([low, block, high], axis=dim)
 
 
 def swish_act(value):
@@ -54,10 +52,15 @@
     return jnp.stack(taps, axis=0)
 
 
-def finish_four(mixed, image_mean, squeeze_down, squeeze_up, project_four):
-    squeezed = swish_act(
-        jnp.dot(image_mean.astype(jnp.bfloat16), squeeze_down, preferred_element_type=jnp.float32)
-    ).astype(jnp.bfloat16)
+def finish_four(mixed, sums, cell_count, squeeze_down, squeeze_up, project_four):
+    group = lax.axis_size("space")
+    part = jnp.dot(sums / cell_count, squeeze_down.astype(jnp.float32), precision="highest")
+    part = jnp.pad(part, ((0, 0), (0, -part.shape[1] % 128)))
+    parts = lax.all_to_all(
+        jnp.broadcast_to(part, (group,) + part.shape), "space", split_axis=0, concat_axis=0
+    )
+    total = jnp.sum(parts, axis=0)[:, : squeeze_down.shape[1]]
+    squeezed = swish_act(total).astype(jnp.bfloat16)
     gate_vals = jax.nn.sigmoid(jnp.dot(squeezed, squeeze_up, preferred_element_type=jnp.float32))
     hidden = (mixed * gate_vals[:, None, None, :]).astype(jnp.bfloat16)
     s, r, w, e = hidden.shape
@@ -90,13 +93,30 @@
     back_spread = depthwise(back_padded, dw_five[::-1], 5)
     back_pre = (back_spread.reshape(-1, chans) * swish_slope(pre_act)).astype(jnp.bfloat16)
     grad_expand = lax.dot_general(
-        flat_rows, back_pre, (((0,), (0,)), ((), ())), preferred_element_type=jnp.float32
+        back_pre, flat_rows, (((0,), (0,)), ((), ())), preferred_element_type=jnp.float32
     )
     back_inputs = lax.dot_general(
         back_pre, expand_five, (((1,), (1,)), ((), ())), preferred_element_type=jnp.float32
     )
     back_inputs = back_inputs.astype(jnp.bfloat16).reshape(s, h, w, c)
-    return (grad_expand * factor, grad_depthwise * factor, grad_project * factor, back_inputs)
+    grads = jnp.concatenate([grad_project, grad_expand, grad_depthwise.T], axis=1) * factor
+    return grads, back_inputs
+
+
+def reduced(grads, width):
+    group, shards = lax.axis_size("space"), lax.axis_size("dp")
+    rows = grads.shape[0]
+    padded = jnp.pad(grads.astype(jnp.bfloat16), ((0, 0), (0, width - grads.shape[1])))
+    padded = padded.reshape(rows, group, width // group).transpose(1, 0, 2)
+    parts = lax.all_to_all(padded, "space", split_axis=0, concat_axis=0)
+    mine = jnp.sum(parts.astype(jnp.float32), axis=0)
+    mine = mine.reshape(shards, rows // shards, width // group)
+    parts = lax.all_to_all(mine, "dp", split_axis=0, concat_axis=0)
+    total = jnp.sum(parts, axis=0)
+    wide = lax.all_to_all(
+        jnp.broadcast_to(total, (group,) + total.shape), "space", split_axis=0, concat_axis=0
+    )
+    return wide.transpose(1, 0, 2).reshape(rows // shards, width)
 
 
 def local(
@@ -113,30 +133,25 @@
     group_size = lax.axis_size("space")
     full_rows = expanded.shape[1] * group_size
     cell_count = full_rows * expanded.shape[2]
-    padded = padded_2(expanded, (("space", 1),), 1)
+    padded = padded_2(expanded, "space", 1, 1)
     mixed = swish_act(depthwise(padded, dw_four, 3))
-    summed = lax.psum(jnp.sum(mixed, axis=(1, 2)), "space")
-    image_mean = summed / cell_count
-    row_out = finish_four(mixed, image_mean, squeeze_down, squeeze_up, project_four)
+    sums = jnp.sum(mixed, axis=(1, 2))
+    row_out = finish_four(mixed, sums, cell_count, squeeze_down, squeeze_up, project_four)
     section_out = lax.all_to_all(row_out, "space", split_axis=0, concat_axis=1, tiled=True)
     total_pixels = (
         cotangent.shape[0] * group_size * lax.axis_size("dp") * full_rows * expanded.shape[2]
     )
     factor = 1.0 / math.sqrt(total_pixels)
-    grad_e, grad_d, grad_p, back_inputs = section_five(
+    grads, back_inputs = section_five(
         section_out, expand_five, dw_five, project_five, cotangent, factor
     )
     input_cotangent = lax.all_to_all(back_inputs, "space", split_axis=1, concat_axis=0, tiled=True)
-    group_e, group_d, group_p = (
-        lax.psum(grad_e.astype(jnp.bfloat16), "space").astype(jnp.float32),
-        lax.psum(grad_d.astype(jnp.bfloat16), "space").astype(jnp.float32),
-        lax.psum(grad_p.astype(jnp.bfloat16), "space").astype(jnp.float32),
-    )
-    grad_e, grad_d, grad_p = (
-        lax.psum_scatter(group_e, "dp", scatter_dimension=1, tiled=True),
-        lax.psum_scatter(group_d, "dp", scatter_dimension=1, tiled=True),
-        lax.psum_scatter(group_p, "dp", scatter_dimension=0, tiled=True),
-    )
+    total = reduced(grads, 1024)
+    c5, c4 = cotangent.shape[3], expand_five.shape[0]
+    taps = dw_five.shape[0]
+    grad_p = total[:, :c5]
+    grad_e = total[:, c5 : c5 + c4].T
+    grad_d = total[:, c5 + c4 : c5 + c4 + taps].T
     return (grad_e, grad_d, grad_p, input_cotangent)
 
 

time: 800 us -> 224 us (0.28); the launches traced: 789 us -> 221 us
  blocking collectives: 533 us -> 37.1 us
  waiting for transfers between devices: 91.5 us -> 46.4 us
  starting transfers between devices: 61.1 us -> 38.8 us
  between operations: 16 us -> 1.54 us
  local copies, waits for them, and re-layouts: 17.6 us -> 29.3 us
    unnamed x2 -> x0, blocking collectives: 468 us -> none
    psum x1 -> x0, waiting for transfers between devices: 79 us -> none  [local(): lax.psum(grad_e.astype(jnp.bfloat16), 'space').astype(jnp.float32)]
    psum x2 -> x0, blocking collectives: 64.9 us -> none  [the longest x1 34.2 us: local(): lax.psum(grad_d.astype(jnp.bfloat16), 'space').astype(jnp.float32)]
    unnamed x16 -> x0, starting transfers between devices: 42.2 us -> none
    all_to_all x0 -> x2, blocking collectives: none -> 37.1 us  [the longest x1 28.6 us: reduced(): parts = lax.all_to_all(padded, 'space', split_axis=0, concat_axis=0)]
    all_to_all x0 -> x2, waiting for transfers between devices: none -> 26.2 us  [the longest x1 21.8 us: reduced(): parts = lax.all_to_all(mine, 'dp', split_axis=0, concat_axis=0)]
    all_to_all x0 -> x2, starting transfers between devices: none -> 21.4 us  [the longest x1 15.7 us: reduced(): parts = lax.all_to_all(mine, 'dp', split_axis=0, concat_axis=0)]
    another operation x26, local copies, waits for them, and re-layouts: 0.34 us -> 15.1 us  [kernel_grad(): return jnp.stack(taps, axis=0)]
  transfers between devices with their start and end apart: 21 -> 6, of which waited for: 5 -> 6; matrix products, arithmetic and copies ran while one was open for 23% -> 2% of each run, Pallas kernels for 0% -> 0%
where the time goes in v1:
time: 224 us; the launch traced here: 221 us
  other arithmetic  55 us (25%)
  waiting for transfers between devices  46.4 us (21%)
  starting transfers between devices  38.8 us (17%)
  blocking collectives  37.1 us (17%)
  local copies, waits for them, and re-layouts  29.3 us (13%)
  matrix products  12.9 us (6%)
    add x2, other arithmetic, depthwise(): summed = summed + window * kernel[i * span_cells + j]  37.1 us
    all_to_all x1, blocking collectives, reduced(): parts = lax.all_to_all(padded, 'space', split_axis=0, concat_axis=0)  28.6 us
    all_to_all x1, waiting for transfers between devices, reduced(): parts = lax.all_to_all(mine, 'dp', split_axis=0, concat_axis=0)  21.8 us
    all_to_all x1, starting transfers between devices, reduced(): parts = lax.all_to_all(mine, 'dp', split_axis=0, concat_axis=0)  15.7 us
    another operation x26, local copies, waits for them, and re-layouts, kernel_grad(): return jnp.stack(taps, axis=0)  15.1 us
    all_to_all x1, blocking collectives, finish_four(): lax.all_to_all(jnp.broadcast_to(part, (group,) + part.shape), 'space', sp...  8.5 us
    reduce_sum x1, other arithmetic, kernel_grad(): taps.append(jnp.sum(window * grad_field, axis=(0, 1, 2)))  6.53 us
    ppermute x1, waiting for transfers between devices, padded_2(): lax.ppermute(lax.slice_in_dim(block, 0, width, axis=dim), axis, backward)  6.03 us
  transfers between devices with their start and end apart: 6, of which 6 were waited for; matrix products, arithmetic and copies ran while one was open for 2% of the time, Pallas kernels for 0%

profile of v1, /device:TPU:6, one launch (start us, length us, event | category | flops | bytes accessed | tf_op | source)
XLA Modules:
  0.0 221.0 jit_solution(18072119973616215444)
XLA Ops:
  1.9 4.3 %collective-permute-start = (bf16[8,1,16,1152]{3,2,1,0:T(8,128)(2,1)S(1)}, bf16[8,1,16,1152]{3,2,1,0:T(8,128)(2,1)S(1)}, u32[]{:S(2)}, u32[]{:S(2)}) collective-permute-start(bf16[8,1,16,1152]{3,2,1,0:T(8,128)(2,1)S(1)} %get-tuple-element.67), channel_id=1, source_target_pairs={{0,1},{1,2},{2,3},{3,4},{4,5},{5,6},{6,7},{8,9},{9,10},{10,11},{11... | collective-permute-start | bytes 884744 | tf_op jit(solution)/shard_map/ppermute | solution.py:13
  9.3 3.3 %collective-permute-done = bf16[8,1,16,1152]{3,2,1,0:T(8,128)(2,1)S(1)} collective-permute-done((bf16[8,1,16,1152]{3,2,1,0:T(8,128)(2,1)S(1)}, bf16[8,1,16,1152]{3,2,1,0:T(8,128)(2,1)S(1)}, u32[]{:S(2)}, u32[]{:S(2)}) %collective-permute-start) | collective-permute-done | bytes 294944 | tf_op jit(solution)/shard_map/ppermute | solution.py:13
  12.6 6.0 %collective-permute-done.1 = bf16[8,1,16,1152]{3,2,1,0:T(8,128)(2,1)S(1)} collective-permute-done((bf16[8,1,16,1152]{3,2,1,0:T(8,128)(2,1)S(1)}, bf16[8,1,16,1152]{3,2,1,0:T(8,128)(2,1)S(1)}, u32[]{:S(2)}, u32[]{:S(2)}) %collective-permute-start.1) | collective-permute-done | bytes 294944 | tf_op jit(solution)/shard_map/ppermute | solution.py:16
  18.7 2.2 fusion.7
  20.9 3.3 %fusion.116 = (f32[8,1152]{1,0:T(8,128)S(1)}, f32[8,4,16,1152]{3,2,1,0:T(8,128)S(1)}) fusion(f32[1152]{0:T(1024)S(1)} %get-tuple-element.63, bf16[8,6,18,1152]{3,2,1,0:T(8,128)(2,1)S(1)} %fusion.7, f32[1152]{0:T(1024)S(1)} %get-tuple-element.64, bf16[8,1,16,1152]{3,2,1,0:T(8,128)(2,1)S(1)} %collective-permute-done.1, ...), kind=kLoop, calls=%fused_computation.261 | loop fusion | flops 19454976 | bytes 11284992 | tf_op jit(solution)/shard_map/reduce_sum | solution.py:138
  24.5 8.5 %all_to_all.41 = f32[8,8,128]{2,1,0:T(8,128)S(1)} all-to-all(f32[8,8,128]{2,1,0:T(8,128)S(1)} %broadcast_in_dim.7), channel_id=1, replica_groups=mesh['dp'=64,'space'=8] {'space'}, dimensions={0} | all-to-all | bytes 65536 | tf_op jit(solution)/shard_map/all_to_all | solution.py:59
  36.0 5.4 %all-to-all-start.1 = ((bf16[8,4,16,344]{3,2,1,0:T(8,128)(2,1)}), bf16[8,4,16,344]{3,2,1,0:T(8,128)(2,1)S(1)}, u32[]{:S(2)}, u32[]{:S(2)}) async-start(bf16[8,4,16,344]{3,2,1,0:T(8,128)(2,1)} %bitcast.1), calls=%async_computation.1 | async-start | bytes 786432 | tf_op jit(solution)/shard_map/all_to_all | solution.py:140
  41.9 4.9 %all-to-all-done.1 = bf16[8,4,16,344]{3,2,1,0:T(8,128)(2,1)S(1)} async-done(((bf16[8,4,16,344]{3,2,1,0:T(8,128)(2,1)}), bf16[8,4,16,344]{3,2,1,0:T(8,128)(2,1)S(1)}, u32[]{:S(2)}, u32[]{:S(2)}) %all-to-all-start.1) | async-done | bytes 352288 | tf_op jit(solution)/shard_map/all_to_all | solution.py:140
  46.9 2.2 %multiply_convert_fusion.1 = (bf16[512,1152]{1,0:T(8,128)(2,1)S(1)}, f32[512,1152]{1,0:T(8,128)}) fusion(bf16[512,344]{1,0:T(8,128)(2,1)S(1)} %bitcast.60, bf16[344,1152]{1,0:T(8,128)(2,1)S(1)} %copy-done.48), kind=kOutput, calls=%fused_computation.201 | convolution fusion | flops 408748032 | bytes 4683776 | tf_op jit(solution)/shard_map/dot_general | solution.py:77
  49.4 8.2 %fusion.31 = f32[1,32,16,1152]{3,2,1,0:T(8,128)S(1)} fusion(f32[1152]{0:T(1024)S(1)} %get-tuple-element.54, f32[1152]{0:T(1024)S(1)} %get-tuple-element.55, f32[1152]{0:T(1024)S(1)} %get-tuple-element.32, f32[1152]{0:T(1024)S(1)} %get-tuple-element.33, f32[1152]{0:T(1024)S(1)} %get-tuple-element.34, f32[1152]{0:T(1024)S(1)} %get-tuple-element.35, ...), kind=kLoop, calls=%fused_computation.127 | loop fusion | flops 43646976 | bytes 9789440 | tf_op jit(solution)/shard_map/add | solution.py:38
  57.6 2.4 %convolution_bitcast_fusion.1 = f32[1152,480]{0,1:T(8,128)} fusion(f32[1,32,16,1152]{3,2,1,0:T(8,128)S(1)} %fusion.31, bf16[1,32,16,480]{3,2,1,0:T(8,128)(2,1)S(1)} %copy-done.49), kind=kOutput, calls=%fused_computation.48 | convolution fusion | flops 569180160 | bytes 5062656 | tf_op jit(solution)/shard_map/dot_general | solution.py:84
  60.0 3.7 %fusion.54 = (f32[1152]{0:T(1024)S(1)}, f32[1152]{0:T(1024)S(1)}, f32[1152]{0:T(1024)S(1)}, f32[1152]{0:T(1024)S(1)}, f32[1152]{0:T(1024)S(1)}, /*index=5*/f32[1...) fusion(bf16[1,32,16,1152]{3,2,1,0:T(8,128)(2,1)S(1)} %bitcast.59, ...), kind=kOutput, calls=%fused_computation.150 | convolution fusion | flops 583327872 | bytes 10034688 | tf_op jit(solution)/shard_map/dot_general | solution.py:87
  63.7 6.5 %fusion.56 = (f32[1152]{0:T(1024)S(1)}, f32[1152]{0:T(1024)S(1)}, f32[1152]{0:T(1024)S(1)}, f32[1152]{0:T(1024)S(1)}, f32[1152]{0:T(1024)S(1)}, /*index=5*/f32[1...) fusion(f32[1,32,16,1152]{3,2,1,0:T(8,128)S(1)} %get-tuple-eleme, ...), kind=kLoop, calls=%fused_computation.152 | loop fusion | flops 31829760 | bytes 3769344 | tf_op jit(solution)/shard_map/reduce_sum | solution.py:51
  86.8 29.0 %fusion.99 = f32[1,32,16,1152]{3,2,1,0:T(8,128)} fusion(f32[1,36,16,1152]{3,2,1,0:T(8,128)} %pad.33, f32[1,32,16,1152]{3,2,1,0:T(8,128)S(1)} %get-tuple-element.71, f32[1152]{0:T(1024)S(1)} %get-tuple-element.54, f32[1152]{0:T(1024)S(1)} %get-tuple-element.55, f32[1152]{0:T(1024)S(1)} %get-tuple-element.32, f32[1152]{0:T(1024)S(1)} %get-tuple-element.33, ...), kind=kLoop, calls=%fused_computation.195 | loop fusion | flops 28901376 | bytes 16975360 | tf_op jit(solution)/shard_map/add | solution.py:38
  115.8 3.2 %fusion.101 = bf16[512,1152]{1,0:T(8,128)(2,1)S(1)} fusion(f32[1,32,16,1152]{3,2,1,0:T(8,128)} %fusion.99, f32[512,1152]{1,0:T(8,128)} %get-tuple-element.70), kind=kLoop, calls=%fused_computation.198 | loop fusion | flops 5308416 | bytes 5898240 | tf_op jit(solution)/shard_map/convert_element_type | solution.py:94
  121.4 1.9 fusion.1
  123.5 28.6 %all_to_all.42 = bf16[8,1152,128]{1,2,0:T(8,128)(2,1)S(1)} all-to-all(bf16[8,1152,128]{1,2,0:T(8,128)(2,1)S(1)} %bitcast.57), channel_id=1, replica_groups=mesh['dp'=64,'space'=8] {'space'}, dimensions={0} | all-to-all | bytes 4718592 | tf_op jit(solution)/shard_map/all_to_all | solution.py:111
  153.5 2.0 reshape.238
  155.5 15.7 %all-to-all-start.3 = ((f32[64,18,128]{2,1,0:T(8,128)}), f32[64,18,128]{2,1,0:T(8,128)S(1)}, u32[]{:S(2)}, u32[]{:S(2)}) async-start(f32[64,18,128]{2,1,0:T(8,128)} %reshape.238), calls=%async_computation.3 | async-start | bytes 1572864 | tf_op jit(solution)/shard_map/all_to_all | solution.py:114
  174.0 21.8 %all-to-all-done.3 = f32[64,18,128]{2,1,0:T(8,128)S(1)} async-done(((f32[64,18,128]{2,1,0:T(8,128)}), f32[64,18,128]{2,1,0:T(8,128)S(1)}, u32[]{:S(2)}, u32[]{:S(2)}) %all-to-all-start.3) | async-done | bytes 589856 | tf_op jit(solution)/shard_map/all_to_all | solution.py:114
  195.7 5.8 %all-to-all-start.5 = ((bf16[1,32,16,344]{3,2,0,1:T(8,128)(2,1)}), bf16[1,32,16,344]{3,2,0,1:T(8,128)(2,1)S(1)}, u32[]{:S(2)}, u32[]{:S(2)}) async-start(bf16[1,32,16,344]{3,2,0,1:T(8,128)(2,1)} %bitcast.17), calls=%async_computation.5 | async-start | bytes 786432 | tf_op jit(solution)/shard_map/all_to_all | solution.py:148
  201.6 5.9 %all-to-all-done.5 = bf16[1,32,16,344]{3,2,0,1:T(8,128)(2,1)S(1)} async-done(((bf16[1,32,16,344]{3,2,0,1:T(8,128)(2,1)}), bf16[1,32,16,344]{3,2,0,1:T(8,128)(2,1)S(1)}, u32[]{:S(2)}, u32[]{:S(2)}) %all-to-all-start.5) | async-done | bytes 352288 | tf_op jit(solution)/shard_map/all_to_all | solution.py:148
  208.2 5.7 %all-to-all-start.4 = ((f32[8,18,128]{2,1,0:T(8,128)}), f32[8,18,128]{2,1,0:T(8,128)S(1)}, u32[]{:S(2)}, u32[]{:S(2)}) async-start(f32[8,18,128]{2,1,0:T(8,128)} %broadcast_in_dim.8), calls=%async_computation.4 | async-start | bytes 196608 | tf_op jit(solution)/shard_map/all_to_all | solution.py:116
  213.9 4.4 %all-to-all-done.4 = f32[8,18,128]{2,1,0:T(8,128)S(1)} async-done(((f32[8,18,128]{2,1,0:T(8,128)}), f32[8,18,128]{2,1,0:T(8,128)S(1)}, u32[]{:S(2)}, u32[]{:S(2)}) %all-to-all-start.4) | async-done | bytes 73760 | tf_op jit(solution)/shard_map/all_to_all | solution.py:116
  (156 shorter events, 34.4 us)
Async XLA Ops:
  0.6 59.3 %copy-start = (bf16[1152,480]{0,1:T(8,128)(2,1)S(1)}, bf16[1152,480]{0,1:T(8,128)(2,1)}, u32[]{:S(2)}) copy-start(bf16[1152,480]{0,1:T(8,128)(2,1)} %param.16) | copy-start | bytes 3317764
  1.8 19.0 %copy-start.1 = (bf16[8,4,16,1152]{3,2,1,0:T(8,128)(2,1)S(1)}, bf16[8,4,16,1152]{3,2,1,0:T(8,128)(2,1)}, u32[]{:S(2)}) copy-start(bf16[8,4,16,1152]{3,2,1,0:T(8,128)(2,1)} %param.9) | copy-start | bytes 3538948
  1.9 10.8 %collective-permute-start = (bf16[8,1,16,1152]{3,2,1,0:T(8,128)(2,1)S(1)}, bf16[8,1,16,1152]{3,2,1,0:T(8,128)(2,1)S(1)}, u32[]{:S(2)}, u32[]{:S(2)}) collective-permute-start(bf16[8,1,16,1152]{3,2,1,0:T(8,128)(2,1)S(1)} %get-tuple-element.67), channel_id=1, source_target_pairs={{0,1},{1,2},{2,3},{3,4},{4,5},{5,6},{6,7},{8,9},{9,10},{10,11},{11... | collective-permute-start | bytes 884744 | tf_op jit(solution)/shard_map/ppermute | solution.py:13
  6.2 12.5 %collective-permute-start.1 = (bf16[8,1,16,1152]{3,2,1,0:T(8,128)(2,1)S(1)}, bf16[8,1,16,1152]{3,2,1,0:T(8,128)(2,1)S(1)}, u32[]{:S(2)}, u32[]{:S(2)}) collective-permute-start(bf16[8,1,16,1152]{3,2,1,0:T(8,128)(2,1)S(1)} %get-tuple-element.68), channel_id=1, source_target_pairs={{1,0},{2,1},{3,2},{4,3},{5,4},{6,5},{7,6},{9,8},{10,9},{11,10},{12... | collective-permute-start | bytes 884744 | tf_op jit(solution)/shard_map/ppermute | solution.py:16
  34.4 12.4 %copy-start.48 = (bf16[344,1152]{1,0:T(8,128)(2,1)S(1)}, bf16[344,1152]{1,0:T(8,128)(2,1)}, u32[]{:S(2)}) copy-start(bf16[344,1152]{1,0:T(8,128)(2,1)} %param.14) | copy-start | bytes 2377732
  36.0 10.8 %all-to-all-start.1 = ((bf16[8,4,16,344]{3,2,1,0:T(8,128)(2,1)}), bf16[8,4,16,344]{3,2,1,0:T(8,128)(2,1)S(1)}, u32[]{:S(2)}, u32[]{:S(2)}) async-start(bf16[8,4,16,344]{3,2,1,0:T(8,128)(2,1)} %bitcast.1), calls=%async_computation.1 | async-start | bytes 786432 | tf_op jit(solution)/shard_map/all_to_all | solution.py:140
  41.8 7.4 %copy-start.8 = (f32[1152]{0:T(1024)}, f32[1152]{0:T(1024)S(1)}, u32[]{:S(2)}) copy-start(f32[1152]{0:T(1024)S(1)} %get-tuple-element.36) | copy-start | bytes 13828
  41.8 7.4 %copy-start.9 = (f32[1152]{0:T(1024)}, f32[1152]{0:T(1024)S(1)}, u32[]{:S(2)}) copy-start(f32[1152]{0:T(1024)S(1)} %get-tuple-element.37) | copy-start | bytes 13828
  41.8 7.4 %copy-start.10 = (f32[1152]{0:T(1024)}, f32[1152]{0:T(1024)S(1)}, u32[]{:S(2)}) copy-start(f32[1152]{0:T(1024)S(1)} %get-tuple-element.38) | copy-start | bytes 13828
  41.8 7.4 %copy-start.11 = (f32[1152]{0:T(1024)}, f32[1152]{0:T(1024)S(1)}, u32[]{:S(2)}) copy-start(f32[1152]{0:T(1024)S(1)} %get-tuple-element.39) | copy-start | bytes 13828
  41.8 7.4 %copy-start.12 = (f32[1152]{0:T(1024)}, f32[1152]{0:T(1024)S(1)}, u32[]{:S(2)}) copy-start(f32[1152]{0:T(1024)S(1)} %get-tuple-element.40) | copy-start | bytes 13828
  41.9 7.4 %copy-start.13 = (f32[1152]{0:T(1024)}, f32[1152]{0:T(1024)S(1)}, u32[]{:S(2)}) copy-start(f32[1152]{0:T(1024)S(1)} %get-tuple-element.41) | copy-start | bytes 13828
  41.9 7.4 %copy-start.14 = (f32[1152]{0:T(1024)}, f32[1152]{0:T(1024)S(1)}, u32[]{:S(2)}) copy-start(f32[1152]{0:T(1024)S(1)} %get-tuple-element.42) | copy-start | bytes 13828
  41.9 7.4 %copy-start.15 = (f32[1152]{0:T(1024)}, f32[1152]{0:T(1024)S(1)}, u32[]{:S(2)}) copy-start(f32[1152]{0:T(1024)S(1)} %get-tuple-element.43) | copy-start | bytes 13828
  41.9 7.4 %copy-start.16 = (f32[1152]{0:T(1024)}, f32[1152]{0:T(1024)S(1)}, u32[]{:S(2)}) copy-start(f32[1152]{0:T(1024)S(1)} %get-tuple-element.44) | copy-start | bytes 13828
  41.9 7.4 %copy-start.17 = (f32[1152]{0:T(1024)}, f32[1152]{0:T(1024)S(1)}, u32[]{:S(2)}) copy-start(f32[1152]{0:T(1024)S(1)} %get-tuple-element.45) | copy-start | bytes 13828
  41.9 7.4 %copy-start.18 = (f32[1152]{0:T(1024)}, f32[1152]{0:T(1024)S(1)}, u32[]{:S(2)}) copy-start(f32[1152]{0:T(1024)S(1)} %get-tuple-element.46) | copy-start | bytes 13828
  41.9 7.4 %copy-start.19 = (f32[1152]{0:T(1024)}, f32[1152]{0:T(1024)S(1)}, u32[]{:S(2)}) copy-start(f32[1152]{0:T(1024)S(1)} %get-tuple-element.47) | copy-start | bytes 13828
  41.9 7.4 %copy-start.20 = (f32[1152]{0:T(1024)}, f32[1152]{0:T(1024)S(1)}, u32[]{:S(2)}) copy-start(f32[1152]{0:T(1024)S(1)} %get-tuple-element.48) | copy-start | bytes 13828
  49.4 8.2 %copy-start.49 = (bf16[1,32,16,480]{3,2,1,0:T(8,128)(2,1)S(1)}, bf16[1,32,16,480]{3,2,1,0:T(8,128)(2,1)}, u32[]{:S(2)}) copy-start(bf16[1,32,16,480]{3,2,1,0:T(8,128)(2,1)} %param.17) | copy-start | bytes 1474564
  152.4 18.8 %copy-start.3 = (bf16[512,1152]{1,0:T(8,128)(2,1)S(1)}, bf16[512,1152]{1,0:T(8,128)(2,1)}, u32[]{:S(2)}) copy-start(bf16[512,1152]{1,0:T(8,128)(2,1)} %copy-done.2) | copy-start | bytes 3538948
  155.5 40.2 %all-to-all-start.3 = ((f32[64,18,128]{2,1,0:T(8,128)}), f32[64,18,128]{2,1,0:T(8,128)S(1)}, u32[]{:S(2)}, u32[]{:S(2)}) async-start(f32[64,18,128]{2,1,0:T(8,128)} %reshape.238), calls=%async_computation.3 | async-start | bytes 1572864 | tf_op jit(solution)/shard_map/all_to_all | solution.py:114
  195.7 11.8 %all-to-all-start.5 = ((bf16[1,32,16,344]{3,2,0,1:T(8,128)(2,1)}), bf16[1,32,16,344]{3,2,0,1:T(8,128)(2,1)S(1)}, u32[]{:S(2)}, u32[]{:S(2)}) async-start(bf16[1,32,16,344]{3,2,0,1:T(8,128)(2,1)} %bitcast.17), calls=%async_computation.5 | async-start | bytes 786432 | tf_op jit(solution)/shard_map/all_to_all | solution.py:148
  208.2 10.1 %all-to-all-start.4 = ((f32[8,18,128]{2,1,0:T(8,128)}), f32[8,18,128]{2,1,0:T(8,128)S(1)}, u32[]{:S(2)}, u32[]{:S(2)}) async-start(f32[8,18,128]{2,1,0:T(8,128)} %broadcast_in_dim.8), calls=%async_computation.4 | async-start | bytes 196608 | tf_op jit(solution)/shard_map/all_to_all | solution.py:116
  (32 other events, 50.0 us)

commit v2 on v1

v2 whole, which is shorter than its diff:
```python
import functools
import math

import jax
import jax.numpy as jnp
import numpy as np
from jax import lax
from jax.experimental import pallas as pl
from jax.experimental.pallas import tpu as pltpu
from jax.sharding import PartitionSpec as P

H, W, LANES, RB = 32, 16, 128, 4
TAPS = 5
Y, Z, CORES, KEEP = 8, 4, 2, 2
GROUP = 8
SEGS = 7
DW_AT = 88
F32, BF16 = jnp.float32, jnp.bfloat16
MESH = pl.DeviceIdType.MESH


def padded_2(block, axis, dim, width):
    count = lax.axis_size(axis)
    forward = [(i, i + 1) for i in range(count - 1)]
    backward = [(target, source) for source, target in forward]
    low = lax.ppermute(
        lax.slice_in_dim(block, block.shape[dim] - width, None, axis=dim), axis, forward
    )
    high = lax.ppermute(lax.slice_in_dim(block, 0, width, axis=dim), axis, backward)
    return jnp.concatenate([low, block, high], axis=dim)


def sigmoid(value):
    return 0.5 * jnp.tanh(0.5 * value) + 0.5


def swish_act(value):
    return value * sigmoid(value)


def depthwise(padded, kernel, span_cells):
    reach_cells = span_cells // 2
    row_count = padded.shape[1] - 2 * reach_cells
    wide_cols = jnp.pad(padded, ((0, 0), (0, 0), (reach_cells, reach_cells), (0, 0)))
    col_count = padded.shape[2]
    summed = jnp.zeros((padded.shape[0], row_count, col_count, padded.shape[3]), jnp.float32)
    for i in range(span_cells):
        for j in range(span_cells):
            window = wide_cols[:, i : i + row_count, j : j + col_count, :].astype(jnp.float32)
            summed = summed + window * kernel[i * span_cells + j]
    return summed


def finish_four(mixed, sums, cell_count, squeeze_down, squeeze_up, project_four):
    group = lax.axis_size("space")
    part = jnp.dot(sums / cell_count, squeeze_down.astype(jnp.float32), precision="highest")
    part = jnp.pad(part, ((0, 0), (0, -part.shape[1] % 128)))
    parts = lax.all_to_all(
        jnp.broadcast_to(part, (group,) + part.shape), "space", split_axis=0, concat_axis=0
    )
    total = jnp.sum(parts, axis=0)[:, : squeeze_down.shape[1]]
    squeezed = swish_act(total).astype(jnp.bfloat16)
    gate_vals = jax.nn.sigmoid(jnp.dot(squeezed, squeeze_up, preferred_element_type=jnp.float32))
    hidden = (mixed * gate_vals[:, None, None, :]).astype(jnp.bfloat16)
    s, r, w, e = hidden.shape
    return (
        jnp.dot(hidden.reshape(-1, e), project_four, preferred_element_type=jnp.float32)
        .astype(jnp.bfloat16)
        .reshape(s, r, w, -1)
    )


def shifted(block, step):
    if step == 0:
        return block
    low, high = block[:, :8], block[:, 8:]
    at = lax.broadcasted_iota(jnp.int32, low.shape, 1)
    low_r = pltpu.roll(low, (-step) % 8, 1)
    high_r = pltpu.roll(high, (-step) % 8, 1)
    if step > 0:
        inside = at < 8 - step
        return jnp.concatenate(
            [jnp.where(inside, low_r, high_r), jnp.where(inside, high_r, 0.0)], axis=1
        )
    inside = at >= -step
    return jnp.concatenate(
        [jnp.where(inside, low_r, 0.0), jnp.where(inside, high_r, low_r)], axis=1
    )


def tile_forward(taps, spread, back_hidden, hidden, back_deep):
    def rows(at, carry):
        r = at * RB
        window = spread[pl.ds(r, RB + 4)]
        total = None
        for j in range(TAPS):
            part = None
            for i in range(TAPS):
                term = window[i : i + RB] * taps[i * TAPS + j]
                part = term if part is None else part + term
            part = shifted(part, j - 2)
            total = part if total is None else total + part
        sig = sigmoid(total)
        swish = total * sig
        hidden[pl.ds(r, RB)] = swish.astype(BF16)
        slope = sig + swish * (1.0 - sig)
        back_deep[pl.ds(r + 2, RB)] = back_hidden[pl.ds(r, RB)] * slope
        return carry

    lax.fori_loop(0, H // RB, rows, 0)


def tile_backward(taps, spread, back_deep, pre, back_pre, grad_taps):
    grad_taps[...] = jnp.zeros_like(grad_taps)

    def rows(at, carry):
        r = at * RB
        window = back_deep[pl.ds(r, RB + 4)]
        mine = spread[pl.ds(r + 2, RB)]
        total = None
        for j in range(TAPS):
            moved = shifted(mine, j - 2)
            part = None
            for i in range(TAPS):
                rows_i = window[TAPS - 1 - i : TAPS - 1 - i + RB]
                term = rows_i * taps[i * TAPS + j]
                part = term if part is None else part + term
                prod = rows_i * moved
                prod = prod[:, :8] + prod[:, 8:]
                prod = (prod[0] + prod[1]) + (prod[2] + prod[3])
                grad_taps[i * TAPS + j] += prod
            part = shifted(part, 2 - j)
            total = part if total is None else total + part
        value = pre[pl.ds(r, RB)]
        sig = sigmoid(value)
        slope = sig + value * sig * (1.0 - sig)
        back_pre[pl.ds(r, RB)] = (total * slope).astype(BF16)
        return carry

    lax.fori_loop(0, H // RB, rows, 0)


def five_kernel(
    s_ref, cot_ref, exp_ref, dw_ref, proj_ref, g_ref, back_ref,
    s_pad, cot_pad, pre, spread, bhid, hid, bdeep, bpre, gtaps, gsq, total,
):
    tiles = exp_ref.shape[1] // LANES
    s_pad[...] = jnp.zeros_like(s_pad)
    cot_pad[...] = jnp.zeros_like(cot_pad)
    s_pad[:, : s_ref.shape[1]] = s_ref[...]
    cot_pad[:, : cot_ref.shape[1]] = cot_ref[...]
    spread[...] = jnp.zeros_like(spread)
    bdeep[...] = jnp.zeros_like(bdeep)
    gsq[...] = jnp.zeros_like(gsq)
    total[...] = jnp.zeros_like(total)
    g_ref[GROUP - 1, GROUP - 1] = jnp.zeros((LANES, LANES), BF16)

    def put(t, q, block):
        b = t * SEGS + q
        g_ref[lax.rem(b, GROUP), lax.div(b, GROUP)] = block.astype(BF16)

    def tile(t, carry):
        lanes = pl.ds(pl.multiple_of(t * LANES, LANES), LANES)
        exp = exp_ref[:, lanes]
        pre_v = jnp.dot(s_pad[...], exp, preferred_element_type=F32)
        pre[...] = pre_v.reshape(H, W, LANES)
        spread[2 : 2 + H] = (
            (pre_v * sigmoid(pre_v)).astype(BF16).astype(F32).reshape(H, W, LANES)
        )
        bh = lax.dot_general(
            cot_pad[...], proj_ref[lanes], (((1,), (1,)), ((), ())), preferred_element_type=F32
        )
        bhid[...] = bh.reshape(H, W, LANES)
        taps = [dw_ref[k : k + 1, lanes].reshape(1, 1, LANES) for k in range(TAPS * TAPS)]
        tile_forward(taps, spread, bhid, hid, bdeep)
        gp = lax.dot_general(
            hid[...].reshape(H * W, LANES), cot_pad[...], (((0,), (0,)), ((), ())),
            preferred_element_type=F32,
        )
        for q in range(4):
            put(t, q, gp[:, q * LANES : (q + 1) * LANES])
        tile_backward(taps, spread, bdeep, pre, bpre, gtaps)
        bp = bpre[...].reshape(H * W, LANES)
        ge = lax.dot_general(
            bp, s_pad[...], (((0,), (0,)), ((), ())), preferred_element_type=F32
        )
        gsq[DW_AT : DW_AT + TAPS * TAPS] = jnp.sum(gtaps[...], axis=1)
        put(t, 4, ge[:, :LANES])
        put(t, 5, ge[:, LANES : 2 * LANES])
        put(t, 6, ge[:, 2 * LANES :] + gsq[...].T)
        total[...] += lax.dot_general(
            bp, exp, (((1,), (1,)), ((), ())), preferred_element_type=F32
        )
        return carry

    lax.fori_loop(0, tiles, tile, 0)
    back_ref[...] = total[...].astype(BF16)


def five(section_out, cot, expand, taps, project):
    pixels, wide4, wide5 = H * W, 3 * LANES, 4 * LANES
    vm = pl.BlockSpec(memory_space=pltpu.VMEM)
    return pl.pallas_call(
        five_kernel,
        out_shape=(
            jax.ShapeDtypeStruct((GROUP, GROUP, LANES, LANES), BF16),
            jax.ShapeDtypeStruct((pixels, wide4), BF16),
        ),
        in_specs=[vm] * 5,
        out_specs=(vm, vm),
        scratch_shapes=[
            pltpu.VMEM((pixels, wide4), BF16),
            pltpu.VMEM((pixels, wide5), BF16),
            pltpu.VMEM((H, W, LANES), F32),
            pltpu.VMEM((H + 4, W, LANES), F32),
            pltpu.VMEM((H, W, LANES), F32),
            pltpu.VMEM((H, W, LANES), BF16),
            pltpu.VMEM((H + 4, W, LANES), F32),
            pltpu.VMEM((H, W, LANES), BF16),
            pltpu.VMEM((TAPS * TAPS, 8, LANES), F32),
            pltpu.VMEM((LANES, LANES), F32),
            pltpu.VMEM((pixels, wide4), F32),
        ],
        compiler_params=pltpu.CompilerParams(vmem_limit_bytes=48 * 1024 * 1024),
        cost_estimate=pl.CostEstimate(
            flops=3_000_000_000, bytes_accessed=8_000_000, transcendentals=1_800_000
        ),
    )(section_out, cot, expand, taps, project)


def exchange(source, landed, send, recv, me, peer, device):
    copy = pltpu.make_async_remote_copy(
        src_ref=source,
        dst_ref=landed.at[me],
        send_sem=send.at[peer],
        recv_sem=recv.at[me],
        device_id=device,
        device_id_type=MESH,
    )
    copy.start()
    return copy


def arrived(source, landed, send, recv, peer, device):
    pltpu.make_async_remote_copy(
        src_ref=source,
        dst_ref=landed.at[peer],
        send_sem=send.at[peer],
        recv_sem=recv.at[peer],
        device_id=device,
        device_id_type=MESH,
    ).wait_recv()


def reduce_kernel(
    scale, g_ref, back_ref, out_ref, cots_ref,
    got1, got2, got3, got4, half, send2, send3, own4, pick,
    s1, r1, s2, r2, s3, r3, s4, r4, s5, r5, s6, r6, local_sem,
):
    dp, sp = lax.axis_index("dp"), lax.axis_index("space")
    core = lax.rem(dp, CORES)
    z = lax.rem(lax.div(dp, CORES), Z)
    y = lax.div(dp, CORES * Z)

    def at_space(other):
        return (dp, other)

    def at_core(other):
        return (dp + other - core, sp)

    def at_z(other):
        return (dp + (other - z) * CORES, sp)

    def at_y(other):
        return (dp + (other - y) * (CORES * Z), sp)

    spaces = [lax.rem(sp + step, GROUP) for step in range(1, GROUP)]
    ys = [lax.rem(y + step, Y) for step in range(1, Y)]
    zs = [lax.rem(z + step, Z) for step in range(1, Z)]
    other = 1 - core

    barrier = pltpu.get_barrier_semaphore()
    everyone = (
        [at_space(p) for p in spaces] + [at_core(other)] + [at_y(p) for p in ys] + [at_z(p) for p in zs]
    )
    for device in everyone:
        pl.semaphore_signal(barrier, inc=1, device_id=device, device_id_type=MESH)
    pl.semaphore_wait(barrier, len(everyone))

    sent = [exchange(g_ref.at[p], got1, s1, r1, sp, p, at_space(p)) for p in spaces]
    rows = back_ref.shape[0] // GROUP
    sent += [
        exchange(back_ref.at[pl.ds(pl.multiple_of(p * rows, rows), rows)], cots_ref, s6, r6, sp, p, at_space(p))
        for p in spaces
    ]
    own = pltpu.make_async_copy(
        back_ref.at[pl.ds(pl.multiple_of(sp * rows, rows), rows)], cots_ref.at[sp], local_sem
    )
    own.start()
    for p in spaces:
        arrived(g_ref.at[p], got1, s1, r1, p, at_space(p))
    hold = LANES // CORES
    for b in range(GROUP):
        total = g_ref[sp, b].astype(F32)
        for p in spaces:
            total += got1[p, b].astype(F32)
        half[0, b] = total[:hold]
        half[1, b] = total[hold:]

    sent.append(exchange(half.at[other], got2, s2, r2, core, other, at_core(other)))
    arrived(half.at[other], got2, s2, r2, other, at_core(other))
    for p in range(Y):
        for b in range(GROUP // 2):
            mine = [
                half[core, 2 * b + e, 8 * p : 8 * p + 8] + got2[other, 2 * b + e, 8 * p : 8 * p + 8]
                for e in range(2)
            ]
            send3[p, b] = jnp.concatenate(mine, axis=0).astype(BF16)

    sent += [exchange(send3.at[p], got3, s3, r3, y, p, at_y(p)) for p in ys]
    for p in ys:
        arrived(send3.at[p], got3, s3, r3, p, at_y(p))
    total = send3[y].astype(F32)
    for p in ys:
        total += got3[p].astype(F32)
    own4[...] = total

    sent += [exchange(own4, got4, s4, r4, z, p, at_z(p)) for p in zs]
    for p in zs:
        arrived(own4, got4, s4, r4, p, at_z(p))
    for p in zs:
        total += got4[p]
    total = (total * scale).reshape(GROUP, 8, LANES)
    mine = total[:, :KEEP]
    for p in range(1, Z):
        mine = jnp.where(z == p, total[:, KEEP * p : KEEP * (p + 1)], mine)
    for b in range(GROUP):
        pick[KEEP * b : KEEP * (b + 1)] = mine[b]

    out_ref[sp] = pick[...]
    sent += [exchange(pick, out_ref, s5, r5, sp, p, at_space(p)) for p in spaces]
    for p in spaces:
        arrived(pick, out_ref, s5, r5, p, at_space(p))
    for p in spaces:
        arrived(back_ref.at[pl.ds(0, rows)], cots_ref, s6, r6, p, at_space(p))
    own.wait()
    for copy in sent:
        copy.wait_send()


def reduced(grads, back, scale):
    vm = pl.BlockSpec(memory_space=pltpu.VMEM)
    dma = pltpu.SemaphoreType.DMA
    sems = [dma((n,)) for n in (GROUP, GROUP, CORES, CORES, Y, Y, Z, Z, GROUP, GROUP, GROUP, GROUP)]
    pixels, wide = back.shape
    return pl.pallas_call(
        functools.partial(reduce_kernel, scale),
        out_shape=(
            jax.ShapeDtypeStruct((GROUP, GROUP * KEEP, LANES), F32),
            jax.ShapeDtypeStruct((GROUP, pixels // GROUP, wide), BF16),
        ),
        in_specs=[vm, vm],
        out_specs=(vm, vm),
        scratch_shapes=[
            pltpu.VMEM((GROUP, GROUP, LANES, LANES), BF16),
            pltpu.VMEM((CORES, GROUP, LANES // CORES, LANES), F32),
            pltpu.VMEM((Y, GROUP // 2, 16, LANES), BF16),
            pltpu.VMEM((Z, GROUP // 2, 16, LANES), F32),
            pltpu.VMEM((CORES, GROUP, LANES // CORES, LANES), F32),
            pltpu.VMEM((CORES, 8, LANES), F32),
            pltpu.VMEM((Y, GROUP // 2, 16, LANES), BF16),
            pltpu.VMEM((GROUP // 2, 16, LANES), F32),
            pltpu.VMEM((GROUP * KEEP, LANES), F32),
            *sems,
            dma(()),
        ],
        compiler_params=pltpu.CompilerParams(
            collective_id=0, has_side_effects=True, vmem_limit_bytes=48 * 1024 * 1024
        ),
    )(grads, back)


def channel_order(channels):
    shards = Y * Z * CORES
    each = channels // shards
    order = np.arange(channels).reshape(Y, Z, CORES, each // KEEP, KEEP)
    return order.transpose(3, 2, 0, 1, 4).reshape(-1)


def local(
    expanded,
    dw_four,
    squeeze_down,
    squeeze_up,
    project_four,
    expand_five,
    dw_five,
    project_five,
    cotangent,
):
    group_size = lax.axis_size("space")
    full_rows = expanded.shape[1] * group_size
    cell_count = full_rows * expanded.shape[2]
    c4, channels = expand_five.shape
    c5 = cotangent.shape[3]
    place = (
        lax.broadcasted_iota(jnp.int32, (channels, channels), 0)
        == jnp.asarray(channel_order(channels), jnp.int32)[None, :]
    )
    expand = jnp.dot(
        jnp.pad(expand_five, ((0, 3 * LANES - c4), (0, 0))), place.astype(BF16)
    )
    project = lax.dot_general(
        place.astype(BF16), jnp.pad(project_five, ((0, 0), (0, 4 * LANES - c5))), (((0,), (0,)), ((), ()))
    )
    taps = jnp.dot(dw_five, place.astype(F32), precision="highest")

    padded = padded_2(expanded, "space", 1, 1)
    mixed = swish_act(depthwise(padded, dw_four, 3))
    sums = jnp.sum(mixed, axis=(1, 2))
    row_out = finish_four(mixed, sums, cell_count, squeeze_down, squeeze_up, project_four)
    section_out = lax.all_to_all(row_out, "space", split_axis=0, concat_axis=1, tiled=True)
    total_pixels = (
        cotangent.shape[0] * group_size * lax.axis_size("dp") * full_rows * expanded.shape[2]
    )
    factor = 1.0 / math.sqrt(total_pixels)
    grads, back = five(
        section_out.reshape(H * W, c4), cotangent.reshape(H * W, c5), expand, taps, project
    )
    total, cots = reduced(grads, back, factor)
    input_cotangent = cots[:, :, :c4].reshape(group_size, expanded.shape[1], W, c4)
    tiles = channels // LANES
    total = total.reshape(GROUP, GROUP, KEEP, LANES).transpose(1, 0, 2, 3)
    total = total.reshape(GROUP * GROUP, KEEP, LANES)[: tiles * SEGS]
    total = total.reshape(tiles, SEGS, KEEP, LANES).transpose(0, 2, 1, 3)
    total = total.reshape(tiles * KEEP, SEGS * LANES)
    grad_p = total[:, :c5]
    grad_e = total[:, 4 * LANES : 4 * LANES + c4].T
    grad_d = total[:, 6 * LANES + DW_AT : 6 * LANES + DW_AT + TAPS * TAPS].T
    return (grad_e, grad_d, grad_p, input_cotangent)


def solution(mesh):
    in_specs = (
        P("dp", "space", None, None),
        P(),
        P(),
        P(),
        P(),
        P(),
        P(),
        P(),
        P(("dp", "space"), None, None, None),
    )
    out_specs = (P(None, "dp"), P(None, "dp"), P("dp", None), P("dp", "space", None, None))
    return jax.shard_map(local, mesh=mesh, in_specs=in_specs, out_specs=out_specs, check_vma=False)
```

time: 224 us -> 137 us (0.61)
  the two profiles are of different devices: /device:TPU:6 before, /device:TPU:1 now
where the time goes in v2:
time: 137 us; the launch traced here: 136 us
  Pallas kernels  86.3 us (63%)
  starting transfers between devices  17.5 us (13%)
  waiting for transfers between devices  9.35 us (7%)
  local copies, waits for them, and re-layouts  8.25 us (6%)
  matrix products  8.1 us (6%)
  other arithmetic  5.69 us (4%)
    pallas_call x1, Pallas kernels, reduced(): pl.pallas_call(functools.partial(reduce_kernel, scale), out_shape=(jax.Sh...  59.3 us
    pallas_call x1, Pallas kernels, five(): pl.pallas_call(five_kernel, out_shape=(jax.ShapeDtypeStruct((GROUP, GROUP...  26.9 us
    all_to_all x1, starting transfers between devices, finish_four(): lax.all_to_all(jnp.broadcast_to(part, (group,) + part.shape), 'space', sp...  8.63 us
    ppermute x1, starting transfers between devices, padded_2(): lax.ppermute(lax.slice_in_dim(block, block.shape[dim] - width, None, axis...  4.09 us
    ppermute x1, waiting for transfers between devices, padded_2(): lax.ppermute(lax.slice_in_dim(block, 0, width, axis=dim), axis, backward)  3.83 us
    all_to_all x1, starting transfers between devices, local(): lax.all_to_all(row_out, 'space', split_axis=0, concat_axis=1, tiled=True)  3.45 us
    reduce_sum x1, other arithmetic, local(): sums = jnp.sum(mixed, axis=(1, 2))  3.3 us
    unnamed x1, matrix products  2.76 us
  transfers between devices with their start and end apart: 4, of which 4 were waited for; matrix products, arithmetic and copies ran while one was open for 6% of the time, Pallas kernels for 0%

profile of v2, /device:TPU:1, one launch (start us, length us, event | category | flops | bytes accessed | tf_op | source)
XLA Modules:
  0.0 136.0 jit_solution(13042177567213548930)
XLA Ops:
  0.6 1.2 fusion.28
  1.8 4.1 %collective-permute-start = (bf16[8,1,16,1152]{3,2,1,0:T(8,128)(2,1)S(1)}, bf16[8,1,16,1152]{3,2,1,0:T(8,128)(2,1)S(1)}, u32[]{:S(2)}, u32[]{:S(2)}) collective-permute-start(bf16[8,1,16,1152]{3,2,1,0:T(8,128)(2,1)S(1)} %get-tuple-element.23), channel_id=1, source_target_pairs={{0,1},{1,2},{2,3},{3,4},{4,5},{5,6},{6,7},{8,9},{9,10},{10,11},{11... | collective-permute-start | bytes 884744 | tf_op jit(solution)/shard_map/ppermute | solution.py:26
  5.9 1.3 collective-permute-start.1
  7.2 1.4 %slice_reduce_fusion.8 = (f32[1152]{0:T(1024)S(1)}, f32[1152]{0:T(1024)S(1)}, f32[1152]{0:T(1024)S(1)}, f32[1152]{0:T(1024)S(1)}, f32[1152]{0:T(1024)S(1)}, /*in...) fusion(f32[9,1152]{1,0:T(8,128)} %param.11), kind=kLoop, calls=%fused_computation.42 | loop fusion | bytes 82944 | tf_op jit(solution)/shard_map/slice | solution.py:50
  8.6 1.0 collective-permute-done
  9.6 3.8 %collective-permute-done.1 = bf16[8,1,16,1152]{3,2,1,0:T(8,128)(2,1)S(1)} collective-permute-done((bf16[8,1,16,1152]{3,2,1,0:T(8,128)(2,1)S(1)}, bf16[8,1,16,1152]{3,2,1,0:T(8,128)(2,1)S(1)}, u32[]{:S(2)}, u32[]{:S(2)}) %collective-permute-start.1) | collective-permute-done | bytes 294944 | tf_op jit(solution)/shard_map/ppermute | solution.py:29
  13.4 2.2 %fusion.8 = bf16[8,6,18,1152]{3,2,1,0:T(8,128)(2,1)S(1)} fusion(bf16[8,1,16,1152]{3,2,1,0:T(8,128)(2,1)S(1)} %collective-permute-done.1, bf16[8,4,16,1152]{3,2,1,0:T(8,128)(2,1)} %param.10, bf16[8,1,16,1152]{3,2,1,0:T(8,128)(2,1)S(1)} %collective-permute-done), kind=kLoop, calls=%fused_computation.12 | loop fusion | flops 11943936 | bytes 3760128 | tf_op jit(solution)/shard_map/concatenate | solution.py:30
  15.6 3.3 %fusion.27 = (f32[8,1152]{1,0:T(8,128)S(1)}, f32[8,4,16,1152]{3,2,1,0:T(8,128)S(1)}) fusion(f32[1152]{0:T(1024)S(1)} %get-tuple-element.19, bf16[8,6,18,1152]{3,2,1,0:T(8,128)(2,1)S(1)} %fusion.8, f32[1152]{0:T(1024)S(1)} %get-tuple-element.20, bf16[8,1,16,1152]{3,2,1,0:T(8,128)(2,1)S(1)} %collective-permute-done.1, ...), kind=kLoop, calls=%fused_computation.49 | loop fusion | flops 19454976 | bytes 11284992 | tf_op jit(solution)/shard_map/reduce_sum | solution.py:420
  19.2 0.7 broadcast_in_dim.2
  19.9 8.6 %all-to-all-start = ((f32[8,8,128]{2,1,0:T(8,128)}), f32[8,8,128]{2,1,0:T(8,128)S(1)}, u32[]{:S(2)}, u32[]{:S(2)}) async-start(f32[8,8,128]{2,1,0:T(8,128)} %broadcast_in_dim.2), calls=%async_computation | async-start | bytes 65536 | tf_op jit(solution)/shard_map/all_to_all | solution.py:58
  28.5 2.7 %fusion.13.dw_ref = f32[25,1152]{1,0:T(8,128)S(1)} fusion(f32[25,1152]{1,0:T(8,128)} %param.16, s32[1152]{0:T(1024)S(1)} %copy-done.8), kind=kOutput, calls=%fused_computation.18 | convolution fusion | flops 399458304 | bytes 235008 | tf_op jit(solution)/shard_map/dot_general | solution.py:416
  31.3 2.4 %all-to-all-done = f32[8,8,128]{2,1,0:T(8,128)S(1)} async-done(((f32[8,8,128]{2,1,0:T(8,128)}), f32[8,8,128]{2,1,0:T(8,128)S(1)}, u32[]{:S(2)}, u32[]{:S(2)}) %all-to-all-start) | async-done | bytes 32800 | tf_op jit(solution)/shard_map/all_to_all | solution.py:58
  34.1 0.7 convolution_convert_fusion.1
  34.7 0.9 copy.19
  35.6 3.5 %all-to-all-start.1 = ((bf16[8,4,16,344]{3,2,1,0:T(8,128)(2,1)}), bf16[8,4,16,344]{3,2,1,0:T(8,128)(2,1)S(1)}, u32[]{:S(2)}, u32[]{:S(2)}) async-start(bf16[8,4,16,344]{3,2,1,0:T(8,128)(2,1)} %bitcast.1), calls=%async_computation.1 | async-start | bytes 786432 | tf_op jit(solution)/shard_map/all_to_all | solution.py:422
  39.1 1.5 %fusion.2.exp_ref = bf16[384,1152]{1,0:T(8,128)(2,1)S(1)} fusion(s32[1152]{0:T(1024)S(1)} %copy-done.8, bf16[344,1152]{1,0:T(8,128)(2,1)S(1)} %copy-done.6), kind=kOutput, calls=%fused_computation.5 | convolution fusion | flops 1020542976 | bytes 1681920 | tf_op jit(solution)/shard_map/dot_general | solution.py:410
  40.7 2.8 %convolution_convert_fusion.proj_ref = bf16[1152,512]{1,0:T(8,128)(2,1)} fusion(s32[1152]{0:T(1024)S(1)} %copy-done.8, bf16[1152,480]{0,1:T(8,128)(2,1)S(1)} %copy-done.5), kind=kOutput, calls=%fused_computation.10 | convolution fusion | flops 1362198528 | bytes 2290176
  43.4 2.2 %all-to-all-done.1 = bf16[8,4,16,344]{3,2,1,0:T(8,128)(2,1)S(1)} async-done(((bf16[8,4,16,344]{3,2,1,0:T(8,128)(2,1)}), bf16[8,4,16,344]{3,2,1,0:T(8,128)(2,1)S(1)}, u32[]{:S(2)}, u32[]{:S(2)}) %all-to-all-start.1) | async-done | bytes 352288 | tf_op jit(solution)/shard_map/all_to_all | solution.py:422
  45.6 1.3 copy-done.2
  46.9 26.9 %shard_map.129 = (bf16[8,8,128,128]{3,2,1,0:T(8,128)(2,1)S(1)}, bf16[512,384]{1,0:T(8,128)(2,1)S(1)}) custom-call(bf16[512,344]{1,0:T(8,128)(2,1)S(1)} %bitcast.32, bf16[512,480]{1,0:T(8,128)(2,1)S(1)} %bitcast.34, bf16[384,1152]{1,0:T(8,128)(2,1)S(1)} %fusion.2.exp_ref, f32[25,1152]{1,0:T(8,128)S(1)} %fusion.13.dw_ref, bf16[1152,512]{1,0:T(8,128)(2,1)S(1)} %copy-done.2), custom_call_target="tpu_custom_call" | custom-call | flops 3000000000 | bytes 8000000 | tf_op jit(solution)/shard_map/pallas_call | solution.py:203
  73.9 59.3 %shard_map.130 = (f32[8,16,128]{2,1,0:T(8,128)S(1)}, bf16[8,64,384]{2,1,0:T(8,128)(2,1)S(1)}) custom-call(bf16[8,8,128,128]{3,2,1,0:T(8,128)(2,1)S(1)} %get-tuple-element.8.g_ref, bf16[512,384]{1,0:T(8,128)(2,1)S(1)} %get-tuple-element.9.back_ref), custom_call_target="tpu_custom_call" | custom-call | tf_op jit(solution)/shard_map/pallas_call | solution.py:356
  133.4 0.6 slice.115
  134.6 0.7 slice_bitcast_fusion.1
  135.3 0.7 copy.27
  (28 shorter events, 1.4 us)
Async XLA Ops:
  0.6 33.4 %copy-start = (bf16[1152,344]{0,1:T(8,128)(2,1)S(1)}, bf16[1152,344]{0,1:T(8,128)(2,1)}, u32[]{:S(2)}) copy-start(bf16[1152,344]{0,1:T(8,128)(2,1)} %param.14) | copy-start | bytes 2377732
  1.8 13.8 %copy-start.3 = (bf16[8,4,16,1152]{3,2,1,0:T(8,128)(2,1)S(1)}, bf16[8,4,16,1152]{3,2,1,0:T(8,128)(2,1)}, u32[]{:S(2)}) copy-start(bf16[8,4,16,1152]{3,2,1,0:T(8,128)(2,1)} %param.10) | copy-start | bytes 3538948
  1.8 7.7 %collective-permute-start = (bf16[8,1,16,1152]{3,2,1,0:T(8,128)(2,1)S(1)}, bf16[8,1,16,1152]{3,2,1,0:T(8,128)(2,1)S(1)}, u32[]{:S(2)}, u32[]{:S(2)}) collective-permute-start(bf16[8,1,16,1152]{3,2,1,0:T(8,128)(2,1)S(1)} %get-tuple-element.23), channel_id=1, source_target_pairs={{0,1},{1,2},{2,3},{3,4},{4,5},{5,6},{6,7},{8,9},{9,10},{10,11},{11... | collective-permute-start | bytes 884744 | tf_op jit(solution)/shard_map/ppermute | solution.py:26
  5.9 7.5 %collective-permute-start.1 = (bf16[8,1,16,1152]{3,2,1,0:T(8,128)(2,1)S(1)}, bf16[8,1,16,1152]{3,2,1,0:T(8,128)(2,1)S(1)}, u32[]{:S(2)}, u32[]{:S(2)}) collective-permute-start(bf16[8,1,16,1152]{3,2,1,0:T(8,128)(2,1)S(1)} %get-tuple-element.24), channel_id=1, source_target_pairs={{1,0},{2,1},{3,2},{4,3},{5,4},{6,5},{7,6},{9,8},{10,9},{11,10},{12... | collective-permute-start | bytes 884744 | tf_op jit(solution)/shard_map/ppermute | solution.py:29
  15.6 3.3 %copy-start.4 = (bf16[1152,86]{0,1:T(8,128)(2,1)S(1)}, bf16[1152,86]{0,1:T(8,128)(2,1)}, u32[]{:S(2)}) copy-start(bf16[1152,86]{0,1:T(8,128)(2,1)} %param.12) | copy-start | bytes 594436
  15.6 12.9 %copy-start.8 = (s32[1152]{0:T(1024)S(1)}, s32[1152]{0:T(1024)}, u32[]{:S(2)}) copy-start(s32[1152]{0:T(1024)} %constant.16.clone) | copy-start | bytes 13828
  15.6 18.0 %copy-start.7 = (bf16[86,1152]{1,0:T(8,128)(2,1)S(1)}, bf16[86,1152]{1,0:T(8,128)(2,1)}, u32[]{:S(2)}) copy-start(bf16[86,1152]{1,0:T(8,128)(2,1)} %param.13) | copy-start | bytes 594436
  19.9 13.7 %all-to-all-start = ((f32[8,8,128]{2,1,0:T(8,128)}), f32[8,8,128]{2,1,0:T(8,128)S(1)}, u32[]{:S(2)}, u32[]{:S(2)}) async-start(f32[8,8,128]{2,1,0:T(8,128)} %broadcast_in_dim.2), calls=%async_computation | async-start | bytes 65536 | tf_op jit(solution)/shard_map/all_to_all | solution.py:58
  34.0 5.1 %copy-start.6 = (bf16[344,1152]{1,0:T(8,128)(2,1)S(1)}, bf16[344,1152]{1,0:T(8,128)(2,1)}, u32[]{:S(2)}) copy-start(bf16[344,1152]{1,0:T(8,128)(2,1)} %param.15) | copy-start | bytes 2377732
  35.6 10.0 %all-to-all-start.1 = ((bf16[8,4,16,344]{3,2,1,0:T(8,128)(2,1)}), bf16[8,4,16,344]{3,2,1,0:T(8,128)(2,1)S(1)}, u32[]{:S(2)}, u32[]{:S(2)}) async-start(bf16[8,4,16,344]{3,2,1,0:T(8,128)(2,1)} %bitcast.1), calls=%async_computation.1 | async-start | bytes 786432 | tf_op jit(solution)/shard_map/all_to_all | solution.py:422
  39.1 1.5 %copy-start.5 = (bf16[1152,480]{0,1:T(8,128)(2,1)S(1)}, bf16[1152,480]{0,1:T(8,128)(2,1)}, u32[]{:S(2)}) copy-start(bf16[1152,480]{0,1:T(8,128)(2,1)} %param.17) | copy-start | bytes 3317764
  40.7 5.0 %copy-start.1 = (bf16[1,32,16,480]{3,2,1,0:T(8,128)(2,1)S(1)}, bf16[1,32,16,480]{3,2,1,0:T(8,128)(2,1)}, u32[]{:S(2)}) copy-start(bf16[1,32,16,480]{3,2,1,0:T(8,128)(2,1)} %param.18) | copy-start | bytes 1474564
  45.6 1.3 copy-start.2

commit v3 on v2

--- a/solution.py
+++ b/solution.py
@@ -140,11 +140,63 @@
     lax.fori_loop(0, H // RB, rows, 0)
 
 
+def exchange(source, landed, send, recv, device):
+    copy = pltpu.make_async_remote_copy(
+        src_ref=source,
+        dst_ref=landed,
+        send_sem=send,
+        recv_sem=recv,
+        device_id=device,
+        device_id_type=MESH,
+    )
+    copy.start()
+    return copy
+
+
+def arrived(source, landed, send, recv, device):
+    pltpu.make_async_remote_copy(
+        src_ref=source,
+        dst_ref=landed,
+        send_sem=send,
+        recv_sem=recv,
+        device_id=device,
+        device_id_type=MESH,
+    ).wait_recv()
+
+
 def five_kernel(
-    s_ref, cot_ref, exp_ref, dw_ref, proj_ref, g_ref, back_ref,
-    s_pad, cot_pad, pre, spread, bhid, hid, bdeep, bpre, gtaps, gsq, total,
+    scale, s_ref, cot_ref, exp_ref, dw_ref, proj_ref, out_ref, cots_ref,
+    s_pad, cot_pad, pre, spread, bhid, hid, bdeep, bpre, gtaps, gsq, total, back,
+    mine, give, got_core, sums, got_space, send_y, got_y, own_z, got_z, pick,
+    core_s, core_r, space_s, space_r, y_s, y_r, z_s, z_r, all_s, all_r, cot_s, cot_r, local_sem,
 ):
+    dp, sp = lax.axis_index("dp"), lax.axis_index("space")
+    core = lax.rem(dp, CORES)
+    z = lax.rem(lax.div(dp, CORES), Z)
+    y = lax.div(dp, CORES * Z)
+    other = 1 - core
+    half = LANES // CORES
     tiles = exp_ref.shape[1] // LANES
+
+    def at_space(place):
+        return (dp, place)
+
+    def at_z(place):
+        return (dp + (place - z) * CORES, sp)
+
+    def at_y(place):
+        return (dp + (place - y) * (CORES * Z), sp)
+
+    sibling = (dp + other - core, sp)
+    spaces = [lax.rem(sp + step, GROUP) for step in range(1, GROUP)]
+    ys = [lax.rem(y + step, Y) for step in range(1, Y)]
+    zs = [lax.rem(z + step, Z) for step in range(1, Z)]
+
+    barrier = pltpu.get_barrier_semaphore()
+    everyone = [at_space(p) for p in spaces] + [sibling] + [at_y(p) for p in ys] + [at_z(p) for p in zs]
+    for device in everyone:
+        pl.semaphore_signal(barrier, inc=1, device_id=device, device_id_type=MESH)
+
     s_pad[...] = jnp.zeros_like(s_pad)
     cot_pad[...] = jnp.zeros_like(cot_pad)
     s_pad[:, : s_ref.shape[1]] = s_ref[...]
@@ -153,11 +205,29 @@
     bdeep[...] = jnp.zeros_like(bdeep)
     gsq[...] = jnp.zeros_like(gsq)
     total[...] = jnp.zeros_like(total)
-    g_ref[GROUP - 1, GROUP - 1] = jnp.zeros((LANES, LANES), BF16)
+    sums[GROUP - 1, GROUP - 1] = jnp.zeros((half, LANES), BF16)
+    pl.semaphore_wait(barrier, len(everyone))
 
     def put(t, q, block):
-        b = t * SEGS + q
-        g_ref[lax.rem(b, GROUP), lax.div(b, GROUP)] = block.astype(BF16)
+        low, high = block[:half], block[half:]
+        mine[t, q] = jnp.where(core == 0, low, high)
+        give[t, q] = jnp.where(core == 0, high, low).astype(BF16)
+
+    def send_block(owner, slot):
+        @pl.when(owner != sp)
+        def _():
+            exchange(
+                sums.at[owner, slot], got_space.at[sp, slot], space_s.at[owner, slot],
+                space_r.at[sp, slot], at_space(owner),
+            )
+
+    def finish(t):
+        arrived(give.at[t], got_core.at[t], core_s.at[t], core_r.at[t], sibling)
+        for q in range(SEGS):
+            b = t * SEGS + q
+            owner, slot = lax.rem(b, GROUP), lax.div(b, GROUP)
+            sums[owner, slot] = (mine[t, q] + got_core[t, q].astype(F32)).astype(BF16)
+            send_block(owner, slot)
 
     def tile(t, carry):
         lanes = pl.ds(pl.multiple_of(t * LANES, LANES), LANES)
@@ -188,23 +258,109 @@
         put(t, 4, ge[:, :LANES])
         put(t, 5, ge[:, LANES : 2 * LANES])
         put(t, 6, ge[:, 2 * LANES :] + gsq[...].T)
+        exchange(give.at[t], got_core.at[t], core_s.at[t], core_r.at[t], sibling)
         total[...] += lax.dot_general(
             bp, exp, (((1,), (1,)), ((), ())), preferred_element_type=F32
         )
+
+        @pl.when(t > 0)
+        def _():
+            finish(t - 1)
+
         return carry
 
     lax.fori_loop(0, tiles, tile, 0)
-    back_ref[...] = total[...].astype(BF16)
-
-
-def five(section_out, cot, expand, taps, project):
+    back[...] = total[...].astype(BF16)
+    finish(tiles - 1)
+    send_block(GROUP - 1, GROUP - 1)
+
+    rows = back.shape[0] // GROUP
+
+    def rows_of(place):
+        return back.at[pl.ds(pl.multiple_of(place * rows, rows), rows)]
+
+    sent = [
+        exchange(rows_of(p), cots_ref.at[sp], cot_s.at[p], cot_r.at[sp], at_space(p))
+        for p in spaces
+    ]
+    own = pltpu.make_async_copy(rows_of(sp), cots_ref.at[sp], local_sem)
+    own.start()
+
+    for b in range(GROUP // 2):
+        pair = []
+        for slot in (2 * b, 2 * b + 1):
+            for p in spaces:
+                arrived(
+                    sums.at[p, slot], got_space.at[p, slot], space_s.at[p, slot],
+                    space_r.at[p, slot], at_space(p),
+                )
+            block = sums[sp, slot].astype(F32)
+            for p in spaces:
+                block += got_space[p, slot].astype(F32)
+            pair.append(block.reshape(Y, 8, LANES))
+        send_y[:, b] = jnp.concatenate(pair, axis=1).astype(BF16)
+
+    sent += [exchange(send_y.at[p], got_y.at[y], y_s.at[p], y_r.at[y], at_y(p)) for p in ys]
+    for p in ys:
+        arrived(send_y.at[p], got_y.at[p], y_s.at[p], y_r.at[p], at_y(p))
+    summed = send_y[y].astype(F32)
+    for p in ys:
+        summed += got_y[p].astype(F32)
+    own_z[...] = summed
+
+    sent += [exchange(own_z, got_z.at[z], z_s.at[p], z_r.at[z], at_z(p)) for p in zs]
+    for p in zs:
+        arrived(own_z, got_z.at[p], z_s.at[p], z_r.at[p], at_z(p))
+    for p in zs:
+        summed += got_z[p]
+    summed = (summed * scale).reshape(GROUP, 8, LANES)
+    kept = summed[:, :KEEP]
+    for p in range(1, Z):
+        kept = jnp.where(z == p, summed[:, KEEP * p : KEEP * (p + 1)], kept)
+    for b in range(GROUP):
+        pick[KEEP * b : KEEP * (b + 1)] = kept[b]
+
+    out_ref[sp] = pick[...]
+    sent += [exchange(pick, out_ref.at[sp], all_s.at[p], all_r.at[sp], at_space(p)) for p in spaces]
+    for p in spaces:
+        arrived(pick, out_ref.at[p], all_s.at[p], all_r.at[p], at_space(p))
+    for p in spaces:
+        arrived(rows_of(p), cots_ref.at[p], cot_s.at[p], cot_r.at[p], at_space(p))
+    own.wait()
+    for copy in sent:
+        copy.wait_send()
+
+    def drain_core(t, carry):
+        pltpu.make_async_remote_copy(
+            src_ref=give.at[t], dst_ref=got_core.at[t], send_sem=core_s.at[t],
+            recv_sem=core_r.at[t], device_id=sibling, device_id_type=MESH,
+        ).wait_send()
+        return carry
+
+    lax.fori_loop(0, tiles, drain_core, 0)
+
+    def drain_space(slot, carry):
+        for p in spaces:
+            pltpu.make_async_remote_copy(
+                src_ref=sums.at[p, slot], dst_ref=got_space.at[sp, slot],
+                send_sem=space_s.at[p, slot], recv_sem=space_r.at[sp, slot],
+                device_id=at_space(p), device_id_type=MESH,
+            ).wait_send()
+        return carry
+
+    lax.fori_loop(0, GROUP, drain_space, 0)
+
+
+def five(section_out, cot, expand, taps, project, scale):
     pixels, wide4, wide5 = H * W, 3 * LANES, 4 * LANES
+    tiles, half = expand.shape[1] // LANES, LANES // CORES
     vm = pl.BlockSpec(memory_space=pltpu.VMEM)
+    dma = pltpu.SemaphoreType.DMA
     return pl.pallas_call(
-        five_kernel,
+        functools.partial(five_kernel, scale),
         out_shape=(
-            jax.ShapeDtypeStruct((GROUP, GROUP, LANES, LANES), BF16),
-            jax.ShapeDtypeStruct((pixels, wide4), BF16),
+            jax.ShapeDtypeStruct((GROUP, GROUP * KEEP, LANES), F32),
+            jax.ShapeDtypeStruct((GROUP, pixels // GROUP, wide4), BF16),
         ),
         in_specs=[vm] * 5,
         out_specs=(vm, vm),
@@ -220,164 +376,38 @@
             pltpu.VMEM((TAPS * TAPS, 8, LANES), F32),
             pltpu.VMEM((LANES, LANES), F32),
             pltpu.VMEM((pixels, wide4), F32),
-        ],
-        compiler_params=pltpu.CompilerParams(vmem_limit_bytes=48 * 1024 * 1024),
-        cost_estimate=pl.CostEstimate(
-            flops=3_000_000_000, bytes_accessed=8_000_000, transcendentals=1_800_000
-        ),
-    )(section_out, cot, expand, taps, project)
-
-
-def exchange(source, landed, send, recv, me, peer, device):
-    copy = pltpu.make_async_remote_copy(
-        src_ref=source,
-        dst_ref=landed.at[me],
-        send_sem=send.at[peer],
-        recv_sem=recv.at[me],
-        device_id=device,
-        device_id_type=MESH,
-    )
-    copy.start()
-    return copy
-
-
-def arrived(source, landed, send, recv, peer, device):
-    pltpu.make_async_remote_copy(
-        src_ref=source,
-        dst_ref=landed.at[peer],
-        send_sem=send.at[peer],
-        recv_sem=recv.at[peer],
-        device_id=device,
-        device_id_type=MESH,
-    ).wait_recv()
-
-
-def reduce_kernel(
-    scale, g_ref, back_ref, out_ref, cots_ref,
-    got1, got2, got3, got4, half, send2, send3, own4, pick,
-    s1, r1, s2, r2, s3, r3, s4, r4, s5, r5, s6, r6, local_sem,
-):
-    dp, sp = lax.axis_index("dp"), lax.axis_index("space")
-    core = lax.rem(dp, CORES)
-    z = lax.rem(lax.div(dp, CORES), Z)
-    y = lax.div(dp, CORES * Z)
-
-    def at_space(other):
-        return (dp, other)
-
-    def at_core(other):
-        return (dp + other - core, sp)
-
-    def at_z(other):
-        return (dp + (other - z) * CORES, sp)
-
-    def at_y(other):
-        return (dp + (other - y) * (CORES * Z), sp)
-
-    spaces = [lax.rem(sp + step, GROUP) for step in range(1, GROUP)]
-    ys = [lax.rem(y + step, Y) for step in range(1, Y)]
-    zs = [lax.rem(z + step, Z) for step in range(1, Z)]
-    other = 1 - core
-
-    barrier = pltpu.get_barrier_semaphore()
-    everyone = (
-        [at_space(p) for p in spaces] + [at_core(other)] + [at_y(p) for p in ys] + [at_z(p) for p in zs]
-    )
-    for device in everyone:
-        pl.semaphore_signal(barrier, inc=1, device_id=device, device_id_type=MESH)
-    pl.semaphore_wait(barrier, len(everyone))
-
-    sent = [exchange(g_ref.at[p], got1, s1, r1, sp, p, at_space(p)) for p in spaces]
-    rows = back_ref.shape[0] // GROUP
-    sent += [
-        exchange(back_ref.at[pl.ds(pl.multiple_of(p * rows, rows), rows)], cots_ref, s6, r6, sp, p, at_space(p))
-        for p in spaces
-    ]
-    own = pltpu.make_async_copy(
-        back_ref.at[pl.ds(pl.multiple_of(sp * rows, rows), rows)], cots_ref.at[sp], local_sem
-    )
-    own.start()
-    for p in spaces:
-        arrived(g_ref.at[p], got1, s1, r1, p, at_space(p))
-    hold = LANES // CORES
-    for b in range(GROUP):
-        total = g_ref[sp, b].astype(F32)
-        for p in spaces:
-            total += got1[p, b].astype(F32)
-        half[0, b] = total[:hold]
-        half[1, b] = total[hold:]
-
-    sent.append(exchange(half.at[other], got2, s2, r2, core, other, at_core(other)))
-    arrived(half.at[other], got2, s2, r2, other, at_core(other))
-    for p in range(Y):
-        for b in range(GROUP // 2):
-            mine = [
-                half[core, 2 * b + e, 8 * p : 8 * p + 8] + got2[other, 2 * b + e, 8 * p : 8 * p + 8]
-                for e in range(2)
-            ]
-            send3[p, b] = jnp.concatenate(mine, axis=0).astype(BF16)
-
-    sent += [exchange(send3.at[p], got3, s3, r3, y, p, at_y(p)) for p in ys]
-    for p in ys:
-        arrived(send3.at[p], got3, s3, r3, p, at_y(p))
-    total = send3[y].astype(F32)
-    for p in ys:
-        total += got3[p].astype(F32)
-    own4[...] = total
-
-    sent += [exchange(own4, got4, s4, r4, z, p, at_z(p)) for p in zs]
-    for p in zs:
-        arrived(own4, got4, s4, r4, p, at_z(p))
-    for p in zs:
-        total += got4[p]
-    total = (total * scale).reshape(GROUP, 8, LANES)
-    mine = total[:, :KEEP]
-    for p in range(1, Z):
-        mine = jnp.where(z == p, total[:, KEEP * p : KEEP * (p + 1)], mine)
-    for b in range(GROUP):
-        pick[KEEP * b : KEEP * (b + 1)] = mine[b]
-
-    out_ref[sp] = pick[...]
-    sent += [exchange(pick, out_ref, s5, r5, sp, p, at_space(p)) for p in spaces]
-    for p in spaces:
-        arrived(pick, out_ref, s5, r5, p, at_space(p))
-    for p in spaces:
-        arrived(back_ref.at[pl.ds(0, rows)], cots_ref, s6, r6, p, at_space(p))
-    own.wait()
-    for copy in sent:
-        copy.wait_send()
-
-
-def reduced(grads, back, scale):
-    vm = pl.BlockSpec(memory_space=pltpu.VMEM)
-    dma = pltpu.SemaphoreType.DMA
-    sems = [dma((n,)) for n in (GROUP, GROUP, CORES, CORES, Y, Y, Z, Z, GROUP, GROUP, GROUP, GROUP)]
-    pixels, wide = back.shape
-    return pl.pallas_call(
-        functools.partial(reduce_kernel, scale),
-        out_shape=(
-            jax.ShapeDtypeStruct((GROUP, GROUP * KEEP, LANES), F32),
-            jax.ShapeDtypeStruct((GROUP, pixels // GROUP, wide), BF16),
-        ),
-        in_specs=[vm, vm],
-        out_specs=(vm, vm),
-        scratch_shapes=[
-            pltpu.VMEM((GROUP, GROUP, LANES, LANES), BF16),
-            pltpu.VMEM((CORES, GROUP, LANES // CORES, LANES), F32),
+            pltpu.VMEM((pixels, wide4), BF16),
+            pltpu.VMEM((tiles, SEGS, half, LANES), F32),
+            pltpu.VMEM((tiles, SEGS, half, LANES), BF16),
+            pltpu.VMEM((tiles, SEGS, half, LANES), BF16),
+            pltpu.VMEM((GROUP, GROUP, half, LANES), BF16),
+            pltpu.VMEM((GROUP, GROUP, half, LANES), BF16),
             pltpu.VMEM((Y, GROUP // 2, 16, LANES), BF16),
-            pltpu.VMEM((Z, GROUP // 2, 16, LANES), F32),
-            pltpu.VMEM((CORES, GROUP, LANES // CORES, LANES), F32),
-            pltpu.VMEM((CORES, 8, LANES), F32),
             pltpu.VMEM((Y, GROUP // 2, 16, LANES), BF16),
             pltpu.VMEM((GROUP // 2, 16, LANES), F32),
+            pltpu.VMEM((Z, GROUP // 2, 16, LANES), F32),
             pltpu.VMEM((GROUP * KEEP, LANES), F32),
-            *sems,
+            dma((tiles,)),
+            dma((tiles,)),
+            dma((GROUP, GROUP)),
+            dma((GROUP, GROUP)),
+            dma((Y,)),
+            dma((Y,)),
+            dma((Z,)),
+            dma((Z,)),
+            dma((GROUP,)),
+            dma((GROUP,)),
+            dma((GROUP,)),
+            dma((GROUP,)),
             dma(()),
         ],
         compiler_params=pltpu.CompilerParams(
             collective_id=0, has_side_effects=True, vmem_limit_bytes=48 * 1024 * 1024
         ),
-    )(grads, back)
+        cost_estimate=pl.CostEstimate(
+            flops=3_000_000_000, bytes_accessed=8_000_000, transcendentals=1_800_000
+        ),
+    )(section_out, cot, expand, taps, project)
 
 
 def channel_order(channels):
@@ -424,10 +454,9 @@
         cotangent.shape[0] * group_size * lax.axis_size("dp") * full_rows * expanded.shape[2]
     )
     factor = 1.0 / math.sqrt(total_pixels)
-    grads, back = five(
-        section_out.reshape(H * W, c4), cotangent.reshape(H * W, c5), expand, taps, project
-    )
-    total, cots = reduced(grads, back, factor)
+    total, cots = five(
+        section_out.reshape(H * W, c4), cotangent.reshape(H * W, c5), expand, taps, project, factor
+    )
     input_cotangent = cots[:, :, :c4].reshape(group_size, expanded.shape[1], W, c4)
     tiles = channels // LANES
     total = total.reshape(GROUP, GROUP, KEEP, LANES).transpose(1, 0, 2, 3)

time: 137 us -> 115 us (0.84)
  the two profiles are of different devices: /device:TPU:1 before, /device:TPU:6 now
where the time goes in v3:
time: 115 us; the launch traced here: 114 us
  Pallas kernels  62.8 us (55%)
  starting transfers between devices  16.2 us (14%)
  waiting for transfers between devices  11.7 us (10%)
  local copies, waits for them, and re-layouts  8.25 us (7%)
  matrix products  8.09 us (7%)
  other arithmetic  5.69 us (5%)
    pallas_call x1, Pallas kernels, five(): pl.pallas_call(functools.partial(five_kernel, scale), out_shape=(jax.Shap...  62.8 us
    ppermute x1, waiting for transfers between devices, padded_2(): lax.ppermute(lax.slice_in_dim(block, 0, width, axis=dim), axis, backward)  6.03 us
    all_to_all x1, starting transfers between devices, local(): lax.all_to_all(row_out, 'space', split_axis=0, concat_axis=1, tiled=True)  5.44 us
    all_to_all x1, starting transfers between devices, finish_four(): lax.all_to_all(jnp.broadcast_to(part, (group,) + part.shape), 'space', sp...  4.51 us
    ppermute x1, starting transfers between devices, padded_2(): lax.ppermute(lax.slice_in_dim(block, block.shape[dim] - width, None, axis...  4.33 us
    reduce_sum x1, other arithmetic, local(): sums = jnp.sum(mixed, axis=(1, 2))  3.3 us
    ppermute x1, waiting for transfers between devices, padded_2(): lax.ppermute(lax.slice_in_dim(block, block.shape[dim] - width, None, axis...  3.13 us
    unnamed x1, matrix products  2.76 us
  transfers between devices with their start and end apart: 4, of which 4 were waited for; matrix products, arithmetic and copies ran while one was open for 7% of the time, Pallas kernels for 0%

profile of v3, /device:TPU:6, one launch (start us, length us, event | category | flops | bytes accessed | tf_op | source)
XLA Modules:
  0.0 113.5 jit_solution(8465105888532851452)
XLA Ops:
  0.6 1.2 %fusion.28 = (bf16[8,1,16,1152]{3,2,1,0:T(8,128)(2,1)S(1)}, bf16[8,1,16,1152]{3,2,1,0:T(8,128)(2,1)S(1)}) fusion(bf16[8,4,16,1152]{3,2,1,0:T(8,128)(2,1)} %param.10), kind=kLoop, calls=%fused_computation.50 | loop fusion | bytes 1179648 | tf_op jit(solution)/shard_map/slice | solution.py:27
  1.8 4.3 %collective-permute-start = (bf16[8,1,16,1152]{3,2,1,0:T(8,128)(2,1)S(1)}, bf16[8,1,16,1152]{3,2,1,0:T(8,128)(2,1)S(1)}, u32[]{:S(2)}, u32[]{:S(2)}) collective-permute-start(bf16[8,1,16,1152]{3,2,1,0:T(8,128)(2,1)S(1)} %get-tuple-element.19), channel_id=1, source_target_pairs={{0,1},{1,2},{2,3},{3,4},{4,5},{5,6},{6,7},{8,9},{9,10},{10,11},{11... | collective-permute-start | bytes 884744 | tf_op jit(solution)/shard_map/ppermute | solution.py:26
  6.2 1.9 %collective-permute-start.1 = (bf16[8,1,16,1152]{3,2,1,0:T(8,128)(2,1)S(1)}, bf16[8,1,16,1152]{3,2,1,0:T(8,128)(2,1)S(1)}, u32[]{:S(2)}, u32[]{:S(2)}) collective-permute-start(bf16[8,1,16,1152]{3,2,1,0:T(8,128)(2,1)S(1)} %get-tuple-element.20), channel_id=1, source_target_pairs={{1,0},{2,1},{3,2},{4,3},{5,4},{6,5},{7,6},{9,8},{10,9},{11,10},{12... | collective-permute-start | bytes 884744 | tf_op jit(solution)/shard_map/ppermute | solution.py:29
  8.1 1.4 %slice_reduce_fusion.8 = (f32[1152]{0:T(1024)S(1)}, f32[1152]{0:T(1024)S(1)}, f32[1152]{0:T(1024)S(1)}, f32[1152]{0:T(1024)S(1)}, f32[1152]{0:T(1024)S(1)}, /*in...) fusion(f32[9,1152]{1,0:T(8,128)} %param.11), kind=kLoop, calls=%fused_computation.42 | loop fusion | bytes 82944 | tf_op jit(solution)/shard_map/slice | solution.py:50
  9.5 3.1 %collective-permute-done = bf16[8,1,16,1152]{3,2,1,0:T(8,128)(2,1)S(1)} collective-permute-done((bf16[8,1,16,1152]{3,2,1,0:T(8,128)(2,1)S(1)}, bf16[8,1,16,1152]{3,2,1,0:T(8,128)(2,1)S(1)}, u32[]{:S(2)}, u32[]{:S(2)}) %collective-permute-start) | collective-permute-done | bytes 294944 | tf_op jit(solution)/shard_map/ppermute | solution.py:26
  12.6 6.0 %collective-permute-done.1 = bf16[8,1,16,1152]{3,2,1,0:T(8,128)(2,1)S(1)} collective-permute-done((bf16[8,1,16,1152]{3,2,1,0:T(8,128)(2,1)S(1)}, bf16[8,1,16,1152]{3,2,1,0:T(8,128)(2,1)S(1)}, u32[]{:S(2)}, u32[]{:S(2)}) %collective-permute-start.1) | collective-permute-done | bytes 294944 | tf_op jit(solution)/shard_map/ppermute | solution.py:29
  18.6 2.2 %fusion.8 = bf16[8,6,18,1152]{3,2,1,0:T(8,128)(2,1)S(1)} fusion(bf16[8,1,16,1152]{3,2,1,0:T(8,128)(2,1)S(1)} %collective-permute-done.1, bf16[8,4,16,1152]{3,2,1,0:T(8,128)(2,1)} %param.10, bf16[8,1,16,1152]{3,2,1,0:T(8,128)(2,1)S(1)} %collective-permute-done), kind=kLoop, calls=%fused_computation.12 | loop fusion | flops 11943936 | bytes 3760128 | tf_op jit(solution)/shard_map/concatenate | solution.py:30
  20.9 3.3 %fusion.27 = (f32[8,1152]{1,0:T(8,128)S(1)}, f32[8,4,16,1152]{3,2,1,0:T(8,128)S(1)}) fusion(f32[1152]{0:T(1024)S(1)} %get-tuple-element.15, bf16[8,6,18,1152]{3,2,1,0:T(8,128)(2,1)S(1)} %fusion.8, f32[1152]{0:T(1024)S(1)} %get-tuple-element.16, bf16[8,1,16,1152]{3,2,1,0:T(8,128)(2,1)S(1)} %collective-permute-done.1, ...), kind=kLoop, calls=%fused_computation.49 | loop fusion | flops 19454976 | bytes 11284992 | tf_op jit(solution)/shard_map/reduce_sum | solution.py:450
  24.5 0.7 broadcast_in_dim.2
  25.1 4.5 %all-to-all-start = ((f32[8,8,128]{2,1,0:T(8,128)}), f32[8,8,128]{2,1,0:T(8,128)S(1)}, u32[]{:S(2)}, u32[]{:S(2)}) async-start(f32[8,8,128]{2,1,0:T(8,128)} %broadcast_in_dim.2), calls=%async_computation | async-start | bytes 65536 | tf_op jit(solution)/shard_map/all_to_all | solution.py:58
  29.6 2.7 %fusion.13.dw_ref = f32[25,1152]{1,0:T(8,128)S(1)} fusion(f32[25,1152]{1,0:T(8,128)} %param.16, s32[1152]{0:T(1024)S(1)} %copy-done.8), kind=kOutput, calls=%fused_computation.18 | convolution fusion | flops 399458304 | bytes 235008 | tf_op jit(solution)/shard_map/dot_general | solution.py:446
  32.4 1.5 %all-to-all-done = f32[8,8,128]{2,1,0:T(8,128)S(1)} async-done(((f32[8,8,128]{2,1,0:T(8,128)}), f32[8,8,128]{2,1,0:T(8,128)S(1)}, u32[]{:S(2)}, u32[]{:S(2)}) %all-to-all-start) | async-done | bytes 32800 | tf_op jit(solution)/shard_map/all_to_all | solution.py:58
  34.3 0.7 convolution_convert_fusion.1
  34.9 0.9 copy.19
  35.8 5.4 %all-to-all-start.1 = ((bf16[8,4,16,344]{3,2,1,0:T(8,128)(2,1)}), bf16[8,4,16,344]{3,2,1,0:T(8,128)(2,1)S(1)}, u32[]{:S(2)}, u32[]{:S(2)}) async-start(bf16[8,4,16,344]{3,2,1,0:T(8,128)(2,1)} %bitcast.1), calls=%async_computation.1 | async-start | bytes 786432 | tf_op jit(solution)/shard_map/all_to_all | solution.py:452
  41.3 1.5 %fusion.2.exp_ref = bf16[384,1152]{1,0:T(8,128)(2,1)S(1)} fusion(s32[1152]{0:T(1024)S(1)} %copy-done.8, bf16[344,1152]{1,0:T(8,128)(2,1)S(1)} %copy-done.6), kind=kOutput, calls=%fused_computation.5 | convolution fusion | flops 1020542976 | bytes 1681920 | tf_op jit(solution)/shard_map/dot_general | solution.py:440
  42.8 2.8 %convolution_convert_fusion.proj_ref = bf16[1152,512]{1,0:T(8,128)(2,1)} fusion(s32[1152]{0:T(1024)S(1)} %copy-done.8, bf16[1152,480]{0,1:T(8,128)(2,1)S(1)} %copy-done.5), kind=kOutput, calls=%fused_computation.10 | convolution fusion | flops 1362198528 | bytes 2290176
  45.6 1.1 all-to-all-done.1
  46.7 1.3 %copy-done.2 = bf16[1152,512]{1,0:T(8,128)(2,1)S(1)} copy-done((bf16[1152,512]{1,0:T(8,128)(2,1)S(1)}, bf16[1152,512]{1,0:T(8,128)(2,1)}, u32[]{:S(2)}) %copy-start.2) | copy-done | bytes 1179672
  47.9 62.8 %shard_map.129 = (f32[8,16,128]{2,1,0:T(8,128)S(1)}, bf16[8,64,384]{2,1,0:T(8,128)(2,1)S(1)}) custom-call(bf16[512,344]{1,0:T(8,128)(2,1)S(1)} %bitcast.32, bf16[512,480]{1,0:T(8,128)(2,1)S(1)} %bitcast.34, bf16[384,1152]{1,0:T(8,128)(2,1)S(1)} %fusion.2.exp_ref, f32[25,1152]{1,0:T(8,128)S(1)} %fusion.13.dw_ref, bf16[1152,512]{1,0:T(8,128)(2,1)S(1)} %copy-done.2), custom_call_target="tpu_custom_call" | custom-call | flops 3000000000 | bytes 8000000 | tf_op jit(solution)/shard_map/pallas_call | solution.py:359
  110.9 0.6 slice.115
  111.5 0.6 slice_bitcast_fusion
  112.1 0.7 slice_bitcast_fusion.1
  112.8 0.7 copy.27
  (27 shorter events, 0.8 us)
Async XLA Ops:
  0.6 33.6 %copy-start = (bf16[1152,344]{0,1:T(8,128)(2,1)S(1)}, bf16[1152,344]{0,1:T(8,128)(2,1)}, u32[]{:S(2)}) copy-start(bf16[1152,344]{0,1:T(8,128)(2,1)} %param.14) | copy-start | bytes 2377732
  1.8 19.0 %copy-start.3 = (bf16[8,4,16,1152]{3,2,1,0:T(8,128)(2,1)S(1)}, bf16[8,4,16,1152]{3,2,1,0:T(8,128)(2,1)}, u32[]{:S(2)}) copy-start(bf16[8,4,16,1152]{3,2,1,0:T(8,128)(2,1)} %param.10) | copy-start | bytes 3538948
  1.8 10.8 %collective-permute-start = (bf16[8,1,16,1152]{3,2,1,0:T(8,128)(2,1)S(1)}, bf16[8,1,16,1152]{3,2,1,0:T(8,128)(2,1)S(1)}, u32[]{:S(2)}, u32[]{:S(2)}) collective-permute-start(bf16[8,1,16,1152]{3,2,1,0:T(8,128)(2,1)S(1)} %get-tuple-element.19), channel_id=1, source_target_pairs={{0,1},{1,2},{2,3},{3,4},{4,5},{5,6},{6,7},{8,9},{9,10},{10,11},{11... | collective-permute-start | bytes 884744 | tf_op jit(solution)/shard_map/ppermute | solution.py:26
  6.2 12.5 %collective-permute-start.1 = (bf16[8,1,16,1152]{3,2,1,0:T(8,128)(2,1)S(1)}, bf16[8,1,16,1152]{3,2,1,0:T(8,128)(2,1)S(1)}, u32[]{:S(2)}, u32[]{:S(2)}) collective-permute-start(bf16[8,1,16,1152]{3,2,1,0:T(8,128)(2,1)S(1)} %get-tuple-element.20), channel_id=1, source_target_pairs={{1,0},{2,1},{3,2},{4,3},{5,4},{6,5},{7,6},{9,8},{10,9},{11,10},{12... | collective-permute-start | bytes 884744 | tf_op jit(solution)/shard_map/ppermute | solution.py:29
  20.8 3.3 %copy-start.4 = (bf16[1152,86]{0,1:T(8,128)(2,1)S(1)}, bf16[1152,86]{0,1:T(8,128)(2,1)}, u32[]{:S(2)}) copy-start(bf16[1152,86]{0,1:T(8,128)(2,1)} %param.12) | copy-start | bytes 594436
  20.9 8.8 %copy-start.8 = (s32[1152]{0:T(1024)S(1)}, s32[1152]{0:T(1024)}, u32[]{:S(2)}) copy-start(s32[1152]{0:T(1024)} %constant.16.clone) | copy-start | bytes 13828
  20.9 13.0 %copy-start.7 = (bf16[86,1152]{1,0:T(8,128)(2,1)S(1)}, bf16[86,1152]{1,0:T(8,128)(2,1)}, u32[]{:S(2)}) copy-start(bf16[86,1152]{1,0:T(8,128)(2,1)} %param.13) | copy-start | bytes 594436
  25.1 8.7 %all-to-all-start = ((f32[8,8,128]{2,1,0:T(8,128)}), f32[8,8,128]{2,1,0:T(8,128)S(1)}, u32[]{:S(2)}, u32[]{:S(2)}) async-start(f32[8,8,128]{2,1,0:T(8,128)} %broadcast_in_dim.2), calls=%async_computation | async-start | bytes 65536 | tf_op jit(solution)/shard_map/all_to_all | solution.py:58
  34.2 7.0 %copy-start.6 = (bf16[344,1152]{1,0:T(8,128)(2,1)S(1)}, bf16[344,1152]{1,0:T(8,128)(2,1)}, u32[]{:S(2)}) copy-start(bf16[344,1152]{1,0:T(8,128)(2,1)} %param.15) | copy-start | bytes 2377732
  35.8 10.8 %all-to-all-start.1 = ((bf16[8,4,16,344]{3,2,1,0:T(8,128)(2,1)}), bf16[8,4,16,344]{3,2,1,0:T(8,128)(2,1)S(1)}, u32[]{:S(2)}, u32[]{:S(2)}) async-start(bf16[8,4,16,344]{3,2,1,0:T(8,128)(2,1)} %bitcast.1), calls=%async_computation.1 | async-start | bytes 786432 | tf_op jit(solution)/shard_map/all_to_all | solution.py:452
  41.3 1.5 %copy-start.5 = (bf16[1152,480]{0,1:T(8,128)(2,1)S(1)}, bf16[1152,480]{0,1:T(8,128)(2,1)}, u32[]{:S(2)}) copy-start(bf16[1152,480]{0,1:T(8,128)(2,1)} %param.17) | copy-start | bytes 3317764
  42.8 3.8 %copy-start.1 = (bf16[1,32,16,480]{3,2,1,0:T(8,128)(2,1)S(1)}, bf16[1,32,16,480]{3,2,1,0:T(8,128)(2,1)}, u32[]{:S(2)}) copy-start(bf16[1,32,16,480]{3,2,1,0:T(8,128)(2,1)} %param.18) | copy-start | bytes 1474564
  46.7 1.3 %copy-start.2 = (bf16[1152,512]{1,0:T(8,128)(2,1)S(1)}, bf16[1152,512]{1,0:T(8,128)(2,1)}, u32[]{:S(2)}) copy-start(bf16[1152,512]{1,0:T(8,128)(2,1)} %convolution_convert_fusion.proj_ref) | copy-start | bytes 3538948

commit v4 on v3

v4 whole, which is shorter than its diff:
```python
import functools
import math

import jax
import jax.numpy as jnp
from jax import lax
from jax.experimental import pallas as pl
from jax.experimental.pallas import tpu as pltpu
from jax.sharding import PartitionSpec as P

H, W, LANES, RB = 32, 16, 128, 4
TAPS = 5
Y, Z, CORES, KEEP = 8, 4, 2, 2
GROUP = 8
CHUNKS = 4
SEGS = 7
DW_AT = 88
F32, BF16 = jnp.float32, jnp.bfloat16
MESH = pl.DeviceIdType.MESH
ACROSS = (((1,), (1,)), ((), ()))


def sigmoid(value):
    return 0.5 * jnp.tanh(0.5 * value) + 0.5


def shifted(block, step):
    if step == 0:
        return block
    low, high = block[:, :8], block[:, 8:]
    at = lax.broadcasted_iota(jnp.int32, low.shape, 1)
    low_r = pltpu.roll(low, (-step) % 8, 1)
    high_r = pltpu.roll(high, (-step) % 8, 1)
    if step > 0:
        inside = at < 8 - step
        return jnp.concatenate(
            [jnp.where(inside, low_r, high_r), jnp.where(inside, high_r, 0.0)], axis=1
        )
    inside = at >= -step
    return jnp.concatenate(
        [jnp.where(inside, low_r, 0.0), jnp.where(inside, high_r, low_r)], axis=1
    )


def tile_forward(taps, spread, back_hidden, hidden, back_deep):
    def rows(at, carry):
        r = at * RB
        window = spread[pl.ds(r, RB + 4)]
        total = None
        for j in range(TAPS):
            part = None
            for i in range(TAPS):
                term = window[i : i + RB] * taps[i * TAPS + j]
                part = term if part is None else part + term
            part = shifted(part, j - 2)
            total = part if total is None else total + part
        sig = sigmoid(total)
        swish = total * sig
        hidden[pl.ds(r, RB)] = swish.astype(BF16)
        slope = sig + swish * (1.0 - sig)
        back_deep[pl.ds(r + 2, RB)] = back_hidden[pl.ds(r, RB)] * slope
        return carry

    lax.fori_loop(0, H // RB, rows, 0, unroll=True)


def tile_backward(taps, spread, back_deep, pre, back_pre, grad_taps):
    grad_taps[...] = jnp.zeros_like(grad_taps)

    def rows(at, carry):
        r = at * RB
        window = back_deep[pl.ds(r, RB + 4)]
        mine = spread[pl.ds(r + 2, RB)]
        total = None
        for j in range(TAPS):
            moved = shifted(mine, j - 2)
            part = None
            for i in range(TAPS):
                rows_i = window[TAPS - 1 - i : TAPS - 1 - i + RB]
                term = rows_i * taps[i * TAPS + j]
                part = term if part is None else part + term
                prod = rows_i * moved
                prod = prod[:, :8] + prod[:, 8:]
                prod = (prod[0] + prod[1]) + (prod[2] + prod[3])
                grad_taps[i * TAPS + j] += prod
            part = shifted(part, 2 - j)
            total = part if total is None else total + part
        value = pre[pl.ds(r, RB)]
        sig = sigmoid(value)
        slope = sig + value * sig * (1.0 - sig)
        back_pre[pl.ds(r * W, RB * W)] = (total * slope).astype(BF16).reshape(RB * W, LANES)
        return carry

    lax.fori_loop(0, H // RB, rows, 0, unroll=True)


def exchange(source, landed, send, recv, device):
    copy = pltpu.make_async_remote_copy(
        src_ref=source,
        dst_ref=landed,
        send_sem=send,
        recv_sem=recv,
        device_id=device,
        device_id_type=MESH,
    )
    copy.start()
    return copy


def arrived(source, landed, send, recv, device):
    pltpu.make_async_remote_copy(
        src_ref=source,
        dst_ref=landed,
        send_sem=send,
        recv_sem=recv,
        device_id=device,
        device_id_type=MESH,
    ).wait_recv()


def four_rows(x, taps, first, count):
    total = None
    for j in range(3):
        part = None
        for i in range(3):
            term = x[first + i : first + i + count] * taps[3 * i + j]
            part = term if part is None else part + term
        part = shifted(part, j - 1)
        total = part if total is None else total + part
    return total


def one_row(x, taps, i):
    total = None
    for j in range(3):
        part = shifted(x * taps[3 * i + j], j - 1)
        total = part if total is None else total + part
    return total


def kernel(
    scale, x_ref, dw4_ref, down_ref, up_ref, p4_ref, e5_ref, dw5_ref, p5_ref, cot_ref, out_ref, cots_ref,
    low, high, mixed, acc, gates, hid4, rows4, down, up, part, got_part, dw_split, exp_ref, dw_ref, offset, places, proj_ref,
    s_pad, cot_pad, pre, spread, bhid, hid, bdeep, bpre, gtaps, gsq, back,
    mine, give, got_core, sums, got_space, send_y, got_y, own_z, got_z, pick,
    halo_s, halo_r, part_s, part_r, sec_s, sec_r,
    core_s, core_r, space_s, space_r, y_s, y_r, z_s, z_r, all_s, all_r, cot_s, cot_r, local_sem,
):
    dp, sp = lax.axis_index("dp"), lax.axis_index("space")
    core = lax.rem(dp, CORES)
    z = lax.rem(lax.div(dp, CORES), Z)
    y = lax.div(dp, CORES * Z)
    other = 1 - core
    half = LANES // CORES

    def at_space(place):
        return (dp, place)

    def at_z(place):
        return (dp + (place - z) * CORES, sp)

    def at_y(place):
        return (dp + (place - y) * (CORES * Z), sp)

    sibling = (dp + other - core, sp)
    spaces = [lax.rem(sp + step, GROUP) for step in range(1, GROUP)]
    ys = [lax.rem(y + step, Y) for step in range(1, Y)]
    zs = [lax.rem(z + step, Z) for step in range(1, Z)]

    barrier = pltpu.get_barrier_semaphore()
    everyone = [at_space(p) for p in spaces] + [sibling] + [at_y(p) for p in ys] + [at_z(p) for p in zs]
    for device in everyone:
        pl.semaphore_signal(barrier, inc=1, device_id=device, device_id_type=MESH)

    images, local_rows = x_ref.shape[:2]
    channels = x_ref.shape[3]
    chunk = images // CHUNKS
    cells = local_rows * W

    @pl.when(sp == 0)
    def _():
        low[...] = jnp.zeros_like(low)

    @pl.when(sp == GROUP - 1)
    def _():
        high[...] = jnp.zeros_like(high)

    pl.semaphore_wait(barrier, len(everyone))

    def down_copy(c):
        part = pl.ds(c * chunk, chunk)
        return pltpu.make_async_remote_copy(
            src_ref=x_ref.at[part, local_rows - 1], dst_ref=low.at[part], send_sem=halo_s.at[0, c],
            recv_sem=halo_r.at[0, c], device_id=(dp, lax.rem(sp + 1, GROUP)), device_id_type=MESH,
        )

    def up_copy(c):
        part = pl.ds(c * chunk, chunk)
        return pltpu.make_async_remote_copy(
            src_ref=x_ref.at[part, 0], dst_ref=high.at[part], send_sem=halo_s.at[1, c],
            recv_sem=halo_r.at[1, c], device_id=(dp, lax.rem(sp + GROUP - 1, GROUP)), device_id_type=MESH,
        )

    @pl.when(sp < GROUP - 1)
    def _():
        for c in range(CHUNKS):
            down_copy(c).start()

    @pl.when(sp > 0)
    def _():
        for c in range(CHUNKS):
            up_copy(c).start()

    def taps4(t):
        at = slice(t * LANES, (t + 1) * LANES)
        return [dw4_ref[k : k + 1, at].reshape(1, 1, LANES) for k in range(9)]

    def swish_rows(value):
        return value * sigmoid(value)

    def folded(rows):
        rows = rows[:, :8] + rows[:, 8:]
        return rows[0] + rows[1]

    def inner(n, carry):
        for t in range(channels // LANES):
            at = slice(t * LANES, (t + 1) * LANES)
            taps = taps4(t)
            x = x_ref[n, :, :, at].astype(F32)
            none = jnp.zeros((1, W, LANES), F32)
            value = four_rows(jnp.concatenate([none, x, none], axis=0), taps, 0, local_rows)
            done = swish_rows(value[1:3])
            mixed[n, 0:1, :, at] = value[0:1]
            mixed[n, 1:3, :, at] = done
            mixed[n, 3:4, :, at] = value[3:4]
            acc[n, :, at] = folded(done)
        return carry

    lax.fori_loop(0, images, inner, 0)

    down[...] = jnp.zeros_like(down)
    down[: down_ref.shape[0]] = down_ref[...]
    up[...] = jnp.zeros_like(up)
    up[: up_ref.shape[0]] = up_ref[...]
    rows4[...] = jnp.zeros_like(rows4)
    cot_pad[...] = jnp.zeros_like(cot_pad)
    cot_pad[:, : cot_ref.shape[1]] = cot_ref[...]
    exp_ref[...] = jnp.zeros_like(exp_ref)
    proj_ref[...] = jnp.zeros_like(proj_ref)
    spread[...] = jnp.zeros_like(spread)
    bdeep[...] = jnp.zeros_like(bdeep)
    gsq[...] = jnp.zeros_like(gsq)
    sums[GROUP - 1, GROUP - 1] = jnp.zeros((half, LANES), BF16)
    dw_split[...] = jnp.zeros_like(dw_split)
    rest = dw5_ref[...]
    for k in range(3):
        top = rest.astype(BF16)
        dw_split[32 * k : 32 * k + TAPS * TAPS] = top
        rest = rest - top.astype(F32)
    tiles = channels // LANES
    each = channels // (Y * Z * CORES)

    at = lax.broadcasted_iota(jnp.int32, (LANES, channels), 0)
    shard = ((at >> 3) & 7) * (Z * CORES) + ((at >> 1) & 3) * CORES + (at >> 6)
    offset[...] = lax.broadcasted_iota(jnp.int32, (LANES, channels), 1) - shard * each - (at & 1)

    def reorder_expand(t, carry):
        lanes = pl.ds(pl.multiple_of(t * LANES, LANES), LANES)
        place = jnp.where(offset[...] == t * KEEP, 1.0, 0.0).astype(BF16)
        places[lanes] = place
        exp = lax.dot_general(e5_ref[...], place, ACROSS, preferred_element_type=F32)
        exp_ref[: e5_ref.shape[0], lanes] = exp.astype(BF16)
        taps = lax.dot_general(dw_split[...], place, ACROSS, preferred_element_type=F32)
        dw_ref[:, lanes] = taps[:32] + taps[32:64] + taps[64:]
        return carry

    lax.fori_loop(0, tiles, reorder_expand, 0)

    for c in range(CHUNKS):

        @pl.when(sp > 0)
        def _():
            down_copy(c).wait_recv()

        @pl.when(sp < GROUP - 1)
        def _():
            up_copy(c).wait_recv()

        def outer(n, carry):
            for t in range(tiles):
                at = slice(t * LANES, (t + 1) * LANES)
                taps = taps4(t)
                above = low[n, :, at].astype(F32).reshape(1, W, LANES)
                below = high[n, :, at].astype(F32).reshape(1, W, LANES)
                first = swish_rows(mixed[n, 0:1, :, at] + one_row(above, taps, 0))
                last = swish_rows(mixed[n, 3:4, :, at] + one_row(below, taps, 2))
                mixed[n, 0:1, :, at] = first
                mixed[n, 3:4, :, at] = last
                acc[n, :, at] += folded(jnp.concatenate([first, last], axis=0))
            return carry

        lax.fori_loop(c * chunk, (c + 1) * chunk, outer, 0)

    mean = jnp.sum(acc[...], axis=1) / (GROUP * cells)
    top = mean.astype(BF16)
    rest = (mean - top.astype(F32)).astype(BF16)
    value = lax.dot_general(top, down[...], ACROSS, preferred_element_type=F32)
    value += lax.dot_general(rest, down[...], ACROSS, preferred_element_type=F32)
    part[...] = value
    sent = [exchange(part, got_part.at[sp], part_s.at[p], part_r.at[sp], at_space(p)) for p in spaces]
    for h in range(3):
        at = slice(h * channels // 3, (h + 1) * channels // 3)
        proj = lax.dot_general(places[at], p5_ref[...], ACROSS, preferred_element_type=F32)
        proj_ref[at, : p5_ref.shape[0]] = proj.astype(BF16)
    for p in spaces:
        arrived(part, got_part.at[p], part_s.at[p], part_r.at[p], at_space(p))
    for p in spaces:
        value += got_part[p]
    squeezed = swish_rows(value).astype(BF16)
    gates[...] = sigmoid(jnp.dot(squeezed, up[...], preferred_element_type=F32))

    for n in range(images):
        gated = mixed[n].reshape(cells, channels) * gates[n : n + 1]
        hid4[n * cells : (n + 1) * cells] = gated.astype(BF16)

    def rows4_of(place):
        return rows4.at[pl.ds(pl.multiple_of(place * cells, cells), cells)]

    def landing(place):
        return s_pad.at[pl.ds(pl.multiple_of(place * cells, cells), cells)]

    part_rows = images * cells // 2
    for h in range(2):
        at = slice(h * part_rows, (h + 1) * part_rows)
        value = lax.dot_general(hid4[at], p4_ref[...], ACROSS, preferred_element_type=F32)
        rows4[at, : p4_ref.shape[0]] = value.astype(BF16)
        for n in range(h * images // 2, (h + 1) * images // 2):

            @pl.when(sp != n)
            def _():
                exchange(
                    rows4.at[n * cells : (n + 1) * cells], landing(sp), sec_s.at[n], sec_r.at[sp], at_space(n)
                )

    mine_at = pl.ds(pl.multiple_of(sp * cells, cells), cells)
    s_pad[mine_at] = rows4[mine_at]

    def back_hidden(t, carry):
        lanes = pl.ds(pl.multiple_of(t * LANES, LANES), LANES)
        bh = lax.dot_general(
            cot_pad[...], proj_ref[lanes], ACROSS, preferred_element_type=F32
        )
        bhid[t] = bh.reshape(H, W, LANES)
        return carry

    lax.fori_loop(0, tiles, back_hidden, 0)
    for p in spaces:
        arrived(rows4_of(p), landing(p), sec_s.at[p], sec_r.at[p], at_space(p))

    def put(t, q, block):
        low, high = block[:half], block[half:]
        mine[t, q] = jnp.where(core == 0, low, high)
        give[t, q] = jnp.where(core == 0, high, low).astype(BF16)

    def send_block(owner, slot):
        @pl.when(owner != sp)
        def _():
            exchange(
                sums.at[owner, slot], got_space.at[sp, slot], space_s.at[owner, slot],
                space_r.at[sp, slot], at_space(owner),
            )

    def finish(t):
        arrived(give.at[t], got_core.at[t], core_s.at[t], core_r.at[t], sibling)
        for q in range(SEGS):
            b = t * SEGS + q
            owner, slot = lax.rem(b, GROUP), lax.div(b, GROUP)
            sums[owner, slot] = (mine[t, q] + got_core[t, q].astype(F32)).astype(BF16)
            send_block(owner, slot)

    def tile(t, carry):
        lanes = pl.ds(pl.multiple_of(t * LANES, LANES), LANES)
        exp = exp_ref[:, lanes]
        pre_v = jnp.dot(s_pad[...], exp, preferred_element_type=F32)
        pre[...] = pre_v.reshape(H, W, LANES)
        spread[2 : 2 + H] = (
            (pre_v * sigmoid(pre_v)).astype(BF16).astype(F32).reshape(H, W, LANES)
        )
        taps = [dw_ref[k : k + 1, lanes].reshape(1, 1, LANES) for k in range(TAPS * TAPS)]
        tile_forward(taps, spread, bhid.at[t], hid, bdeep)
        gp = lax.dot_general(
            hid[...].reshape(H * W, LANES), cot_pad[...], (((0,), (0,)), ((), ())),
            preferred_element_type=F32,
        )
        for q in range(4):
            put(t, q, gp[:, q * LANES : (q + 1) * LANES])
        tile_backward(taps, spread, bdeep, pre, bpre.at[:, lanes], gtaps)
        bp = bpre[:, lanes]
        ge = lax.dot_general(
            bp, s_pad[...], (((0,), (0,)), ((), ())), preferred_element_type=F32
        )
        gsq[DW_AT : DW_AT + TAPS * TAPS] = jnp.sum(gtaps[...], axis=1)
        put(t, 4, ge[:, :LANES])
        put(t, 5, ge[:, LANES : 2 * LANES])
        put(t, 6, ge[:, 2 * LANES :] + gsq[...].T)
        exchange(give.at[t], got_core.at[t], core_s.at[t], core_r.at[t], sibling)

        @pl.when(t > 0)
        def _():
            finish(t - 1)

        return carry

    lax.fori_loop(0, tiles, tile, 0)
    back[...] = lax.dot_general(
        bpre[...], exp_ref[...], ACROSS, preferred_element_type=F32
    ).astype(BF16)
    finish(tiles - 1)
    send_block(GROUP - 1, GROUP - 1)

    rows = back.shape[0] // GROUP

    def rows_of(place):
        return back.at[pl.ds(pl.multiple_of(place * rows, rows), rows)]

    sent += [
        exchange(rows_of(p), cots_ref.at[sp], cot_s.at[p], cot_r.at[sp], at_space(p))
        for p in spaces
    ]
    own = pltpu.make_async_copy(rows_of(sp), cots_ref.at[sp], local_sem)
    own.start()

    for b in range(GROUP // 2):
        pair = []
        for slot in (2 * b, 2 * b + 1):
            for p in spaces:
                arrived(
                    sums.at[p, slot], got_space.at[p, slot], space_s.at[p, slot],
                    space_r.at[p, slot], at_space(p),
                )
            block = sums[sp, slot].astype(F32)
            for p in spaces:
                block += got_space[p, slot].astype(F32)
            pair.append(block.reshape(Y, 8, LANES))
        send_y[:, b] = jnp.concatenate(pair, axis=1).astype(BF16)

    sent += [exchange(send_y.at[p], got_y.at[y], y_s.at[p], y_r.at[y], at_y(p)) for p in ys]
    for p in ys:
        arrived(send_y.at[p], got_y.at[p], y_s.at[p], y_r.at[p], at_y(p))
    summed = send_y[y].astype(F32)
    for p in ys:
        summed += got_y[p].astype(F32)
    own_z[...] = summed

    sent += [exchange(own_z, got_z.at[z], z_s.at[p], z_r.at[z], at_z(p)) for p in zs]
    for p in zs:
        arrived(own_z, got_z.at[p], z_s.at[p], z_r.at[p], at_z(p))
    for p in zs:
        summed += got_z[p]
    summed = (summed * scale).reshape(GROUP, 8, LANES)
    kept = summed[:, :KEEP]
    for p in range(1, Z):
        kept = jnp.where(z == p, summed[:, KEEP * p : KEEP * (p + 1)], kept)
    for b in range(GROUP):
        pick[KEEP * b : KEEP * (b + 1)] = kept[b]

    out_ref[sp] = pick[...]
    sent += [exchange(pick, out_ref.at[sp], all_s.at[p], all_r.at[sp], at_space(p)) for p in spaces]
    for p in spaces:
        arrived(pick, out_ref.at[p], all_s.at[p], all_r.at[p], at_space(p))
    for p in spaces:
        arrived(rows_of(p), cots_ref.at[p], cot_s.at[p], cot_r.at[p], at_space(p))
    own.wait()
    for copy in sent:
        copy.wait_send()

    def drain_core(t, carry):
        pltpu.make_async_remote_copy(
            src_ref=give.at[t], dst_ref=got_core.at[t], send_sem=core_s.at[t],
            recv_sem=core_r.at[t], device_id=sibling, device_id_type=MESH,
        ).wait_send()
        return carry

    lax.fori_loop(0, tiles, drain_core, 0)

    def drain_space(slot, carry):
        for p in spaces:
            pltpu.make_async_remote_copy(
                src_ref=sums.at[p, slot], dst_ref=got_space.at[sp, slot],
                send_sem=space_s.at[p, slot], recv_sem=space_r.at[sp, slot],
                device_id=at_space(p), device_id_type=MESH,
            ).wait_send()
        return carry

    lax.fori_loop(0, GROUP, drain_space, 0)
    for p in spaces:
        pltpu.make_async_remote_copy(
            src_ref=rows4_of(p), dst_ref=landing(sp), send_sem=sec_s.at[p], recv_sem=sec_r.at[sp],
            device_id=at_space(p), device_id_type=MESH,
        ).wait_send()

    @pl.when(sp < GROUP - 1)
    def _():
        for c in range(CHUNKS):
            down_copy(c).wait_send()

    @pl.when(sp > 0)
    def _():
        for c in range(CHUNKS):
            up_copy(c).wait_send()


def local(
    expanded,
    dw_four,
    squeeze_down,
    squeeze_up,
    project_four,
    expand_five,
    dw_five,
    project_five,
    cotangent,
):
    images, local_rows, _, channels = expanded.shape
    c4, c5 = expand_five.shape[0], cotangent.shape[3]
    pixels, wide4, wide5 = H * W, 3 * LANES, 4 * LANES
    tiles, half = channels // LANES, LANES // CORES
    total_pixels = images * lax.axis_size("dp") * pixels
    vm = pl.BlockSpec(memory_space=pltpu.VMEM)
    dma = pltpu.SemaphoreType.DMA
    vmem = pltpu.VMEM
    total, cots = pl.pallas_call(
        functools.partial(kernel, 1.0 / math.sqrt(total_pixels)),
        out_shape=(
            jax.ShapeDtypeStruct((GROUP, GROUP * KEEP, LANES), F32),
            jax.ShapeDtypeStruct((GROUP, pixels // GROUP, wide4), BF16),
        ),
        in_specs=[vm] * 9,
        out_specs=(vm, vm),
        scratch_shapes=[
            vmem((images, W, channels), BF16),
            vmem((images, W, channels), BF16),
            vmem(expanded.shape, F32),
            vmem((images, 8, channels), F32),
            vmem((images, channels), F32),
            vmem((pixels, channels), BF16),
            vmem((pixels, wide4), BF16),
            vmem((LANES, channels), BF16),
            vmem((LANES, channels), BF16),
            vmem((images, LANES), F32),
            vmem((GROUP, images, LANES), F32),
            vmem((96, channels), BF16),
            vmem((wide4, channels), BF16),
            vmem((32, channels), F32),
            vmem((LANES, channels), jnp.int32),
            vmem((channels, channels), BF16),
            vmem((channels, wide5), BF16),
            vmem((pixels, wide4), BF16),
            vmem((pixels, wide5), BF16),
            vmem((H, W, LANES), F32),
            vmem((H + 4, W, LANES), F32),
            vmem((tiles, H, W, LANES), F32),
            vmem((H, W, LANES), BF16),
            vmem((H + 4, W, LANES), F32),
            vmem((pixels, channels), BF16),
            vmem((TAPS * TAPS, 8, LANES), F32),
            vmem((LANES, LANES), F32),
            vmem((pixels, wide4), BF16),
            vmem((tiles, SEGS, half, LANES), F32),
            vmem((tiles, SEGS, half, LANES), BF16),
            vmem((tiles, SEGS, half, LANES), BF16),
            vmem((GROUP, GROUP, half, LANES), BF16),
            vmem((GROUP, GROUP, half, LANES), BF16),
            vmem((Y, GROUP // 2, 16, LANES), BF16),
            vmem((Y, GROUP // 2, 16, LANES), BF16),
            vmem((GROUP // 2, 16, LANES), F32),
            vmem((Z, GROUP // 2, 16, LANES), F32),
            vmem((GROUP * KEEP, LANES), F32),
            dma((2, CHUNKS)),
            dma((2, CHUNKS)),
            dma((GROUP,)),
            dma((GROUP,)),
            dma((GROUP,)),
            dma((GROUP,)),
            dma((tiles,)),
            dma((tiles,)),
            dma((GROUP, GROUP)),
            dma((GROUP, GROUP)),
            dma((Y,)),
            dma((Y,)),
            dma((Z,)),
            dma((Z,)),
            dma((GROUP,)),
            dma((GROUP,)),
            dma((GROUP,)),
            dma((GROUP,)),
            dma(()),
        ],
        compiler_params=pltpu.CompilerParams(
            collective_id=0, has_side_effects=True, vmem_limit_bytes=56 * 1024 * 1024
        ),
        cost_estimate=pl.CostEstimate(
            flops=3_000_000_000, bytes_accessed=8_000_000, transcendentals=2_400_000
        ),
    )(
        expanded, dw_four, squeeze_down.T, squeeze_up, project_four.T, expand_five, dw_five, project_five.T,
        cotangent.reshape(pixels, c5),
    )
    input_cotangent = cots[:, :, :c4].reshape(images, local_rows, W, c4)
    total = total.reshape(GROUP, GROUP, KEEP, LANES).transpose(1, 0, 2, 3)
    total = total.reshape(GROUP * GROUP, KEEP, LANES)[: tiles * SEGS]
    total = total.reshape(tiles, SEGS, KEEP, LANES).transpose(0, 2, 1, 3)
    total = total.reshape(tiles * KEEP, SEGS * LANES)
    grad_p = total[:, :c5]
    grad_e = total[:, 4 * LANES : 4 * LANES + c4].T
    grad_d = total[:, 6 * LANES + DW_AT : 6 * LANES + DW_AT + TAPS * TAPS].T
    return (grad_e, grad_d, grad_p, input_cotangent)


def solution(mesh):
    in_specs = (
        P("dp", "space", None, None),
        P(),
        P(),
        P(),
        P(),
        P(),
        P(),
        P(),
        P(("dp", "space"), None, None, None),
    )
    out_specs = (P(None, "dp"), P(None, "dp"), P("dp", None), P("dp", "space", None, None))
    return jax.shard_map(local, mesh=mesh, in_specs=in_specs, out_specs=out_specs, check_vma=False)
```

time: 115 us -> 86.8 us (0.75); the launches traced: 114 us -> 86.7 us
  Pallas kernels: 62.8 us -> 82.3 us
  starting transfers between devices: 16.2 us -> 0 us
  waiting for transfers between devices: 11.7 us -> 0 us
  matrix products: 8.09 us -> 0 us
  other arithmetic: 5.69 us -> 0 us
  local copies, waits for them, and re-layouts: 8.25 us -> 3.67 us
    pallas_call x1, Pallas kernels: 62.8 us -> 82.3 us  [local(): pl.pallas_call(functools.partial(kernel, 1.0 / math.sqrt(total_pixels)),...]
    all_to_all x2 -> x0, starting transfers between devices: 9.95 us -> none  [the longest x1 5.44 us: local(): lax.all_to_all(row_out, 'space', split_axis=0, concat_axis=1, tiled=True)]
    ppermute x2 -> x0, waiting for transfers between devices: 9.16 us -> none  [the longest x1 6.03 us: padded_2(): lax.ppermute(lax.slice_in_dim(block, 0, width, axis=dim), axis, backward)]
    ppermute x2 -> x0, starting transfers between devices: 6.25 us -> none  [the longest x1 4.33 us: padded_2(): lax.ppermute(lax.slice_in_dim(block, block.shape[dim] - width, None, axis...]
    dot_general x5 -> x0, matrix products: 5.33 us -> none  [the longest x1 2.73 us: local(): taps = jnp.dot(dw_five, place.astype(F32), precision='highest')]
    reduce_sum x2 -> x0, other arithmetic: 3.31 us -> none  [the longest x1 3.3 us: local(): sums = jnp.sum(mixed, axis=(1, 2))]
    unnamed x1 -> x0, matrix products: 2.76 us -> none
    slice x2 -> x0, local copies, waits for them, and re-layouts: 2.56 us -> none  [the longest x1 1.38 us: depthwise(): summed = summed + window * kernel[i * span_cells + j]]
  transfers between devices with their start and end apart: 4 -> 0, of which waited for: 4 -> 0; matrix products, arithmetic and copies ran while one was open for 7% -> 0% of each run, Pallas kernels for 0% -> 0%
where the time goes in v4:
time: 86.8 us; the launch traced here: 86.7 us
  Pallas kernels  82.3 us (95%)
  local copies, waits for them, and re-layouts  3.67 us (4%)
    pallas_call x1, Pallas kernels, local(): pl.pallas_call(functools.partial(kernel, 1.0 / math.sqrt(total_pixels)),...  82.3 us

profile of v4, /device:TPU:6, one launch (start us, length us, event | category | flops | bytes accessed | tf_op | source)
XLA Modules:
  0.0 86.7 jit_solution(374343482678053702)
XLA Ops:
  0.6 82.3 %shard_map.120 = (f32[8,16,128]{2,1,0:T(8,128)}, bf16[8,64,384]{2,1,0:T(8,128)(2,1)}) custom-call(bf16[8,4,16,1152]{3,2,1,0:T(8,128)(2,1)} %x_ref.1, f32[9,1152]{1,0:T(8,128)} %dw4_ref.1, bf16[86,1152]{1,0:T(8,128)(2,1)} %bitcast.36, bf16[86,1152]{1,0:T(8,128)(2,1)} %up_ref.1, bf16[344,1152]{1,0:T(8,128)(2,1)} %bitcast.34, bf16[344,1152]{1,0:T(8,128)(2,1)} %e5_ref.1, ...), custom_call_target="tpu_custom_call" | custom-call | flops 3000000000 | bytes 8000000 | tf_op jit(solution)/shard_map/pallas_call | solution.py:532
  83.0 0.0 copy-start
  83.0 0.9 %copy.18 = f32[8,8,2,128]{3,0,1,2:T(8,128)S(1)} copy(f32[8,8,2,128]{3,2,1,0:T(2,128)} %bitcast.32) | data formatting | bytes 131072 | tf_op jit(solution)/shard_map/reshape | solution.py:610
  83.9 0.1 copy.14
  84.0 0.7 slice_bitcast_fusion.1
  84.7 0.6 slice_bitcast_fusion
  85.3 0.6 slice.23
  86.0 0.0 copy-done
  86.0 0.7 copy.20
  (3 shorter events, 0.0 us)
Async XLA Ops:
  83.0 3.0 %copy-start = (bf16[8,64,384]{2,1,0:T(8,128)(2,1)S(1)}, bf16[8,64,384]{2,1,0:T(8,128)(2,1)}, u32[]{:S(2)}) copy-start(bf16[8,64,384]{2,1,0:T(8,128)(2,1)} %get-tuple-element.7) | copy-start | bytes 1179652

commit v5 on v4

--- a/solution.py
+++ b/solution.py
@@ -12,6 +12,7 @@
 TAPS = 5
 Y, Z, CORES, KEEP = 8, 4, 2, 2
 GROUP = 8
+X = 4
 CHUNKS = 4
 SEGS = 7
 DW_AT = 88
@@ -139,10 +140,11 @@
 
 
 def kernel(
-    scale, x_ref, dw4_ref, down_ref, up_ref, p4_ref, e5_ref, dw5_ref, p5_ref, cot_ref, out_ref, cots_ref,
+    scale, x_hbm, dw4_hbm, down_hbm, up_hbm, p4_hbm, e5_hbm, dw5_hbm, p5_hbm, cot_hbm, out_ref, cots_ref,
+    x_ref, dw4_ref, down_ref, up_ref, p4_ref, e5_ref, dw5_ref, p5_ref, cot_ref, fetch,
     low, high, mixed, acc, gates, hid4, rows4, down, up, part, got_part, dw_split, exp_ref, dw_ref, offset, places, proj_ref,
     s_pad, cot_pad, pre, spread, bhid, hid, bdeep, bpre, gtaps, gsq, back,
-    mine, give, got_core, sums, got_space, send_y, got_y, own_z, got_z, pick,
+    mine, give, got_core, sums, got_space, send_y, got_y, send_z, got_z, pick, got_x,
     halo_s, halo_r, part_s, part_r, sec_s, sec_r,
     core_s, core_r, space_s, space_r, y_s, y_r, z_s, z_r, all_s, all_r, cot_s, cot_r, local_sem,
 ):
@@ -156,8 +158,11 @@
     def at_space(place):
         return (dp, place)
 
-    def at_z(place):
-        return (dp + (place - z) * CORES, sp)
+    def at_line(place):
+        return (dp + (place[0] - z) * CORES, place[1] * X + x)
+
+    def at_x(place):
+        return (dp, z_lo * X + place)
 
     def at_y(place):
         return (dp + (place - y) * (CORES * Z), sp)
@@ -166,11 +171,29 @@
     spaces = [lax.rem(sp + step, GROUP) for step in range(1, GROUP)]
     ys = [lax.rem(y + step, Y) for step in range(1, Y)]
     zs = [lax.rem(z + step, Z) for step in range(1, Z)]
+    x, z_lo = lax.rem(sp, X), lax.div(sp, X)
+    xs = [lax.rem(x + step, X) for step in range(1, X)]
+    line = [(z, 1 - z_lo)] + [(p, e) for p in zs for e in range(GROUP // X)]
 
     barrier = pltpu.get_barrier_semaphore()
-    everyone = [at_space(p) for p in spaces] + [sibling] + [at_y(p) for p in ys] + [at_z(p) for p in zs]
+    everyone = [at_space(p) for p in spaces] + [sibling] + [at_y(p) for p in ys] + [at_line(p) for p in line[1:]]
     for device in everyone:
         pl.semaphore_signal(barrier, inc=1, device_id=device, device_id_type=MESH)
+
+    def fetched(k, source, target):
+        copy = pltpu.make_async_copy(source, target, fetch.at[k])
+        copy.start()
+        return copy
+
+    x_in = fetched(0, x_hbm, x_ref)
+    dw4_in = fetched(1, dw4_hbm, dw4_ref)
+    e5_in = fetched(2, e5_hbm, e5_ref)
+    dw5_in = fetched(3, dw5_hbm, dw5_ref)
+    p5_in = fetched(4, p5_hbm, p5_ref)
+    down_in = fetched(5, down_hbm, down_ref)
+    up_in = fetched(6, up_hbm, up_ref)
+    p4_in = fetched(7, p4_hbm, p4_ref)
+    cot_in = fetched(8, cot_hbm, cot_ref)
 
     images, local_rows = x_ref.shape[:2]
     channels = x_ref.shape[3]
@@ -190,14 +213,14 @@
     def down_copy(c):
         part = pl.ds(c * chunk, chunk)
         return pltpu.make_async_remote_copy(
-            src_ref=x_ref.at[part, local_rows - 1], dst_ref=low.at[part], send_sem=halo_s.at[0, c],
+            src_ref=x_hbm.at[part, local_rows - 1], dst_ref=low.at[part], send_sem=halo_s.at[0, c],
             recv_sem=halo_r.at[0, c], device_id=(dp, lax.rem(sp + 1, GROUP)), device_id_type=MESH,
         )
 
     def up_copy(c):
         part = pl.ds(c * chunk, chunk)
         return pltpu.make_async_remote_copy(
-            src_ref=x_ref.at[part, 0], dst_ref=high.at[part], send_sem=halo_s.at[1, c],
+            src_ref=x_hbm.at[part, 0], dst_ref=high.at[part], send_sem=halo_s.at[1, c],
             recv_sem=halo_r.at[1, c], device_id=(dp, lax.rem(sp + GROUP - 1, GROUP)), device_id_type=MESH,
         )
 
@@ -210,6 +233,9 @@
     def _():
         for c in range(CHUNKS):
             up_copy(c).start()
+
+    x_in.wait()
+    dw4_in.wait()
 
     def taps4(t):
         at = slice(t * LANES, (t + 1) * LANES)
@@ -238,6 +264,11 @@
 
     lax.fori_loop(0, images, inner, 0)
 
+    e5_in.wait()
+    dw5_in.wait()
+    down_in.wait()
+    up_in.wait()
+    cot_in.wait()
     down[...] = jnp.zeros_like(down)
     down[: down_ref.shape[0]] = down_ref[...]
     up[...] = jnp.zeros_like(up)
@@ -308,6 +339,7 @@
     value += lax.dot_general(rest, down[...], ACROSS, preferred_element_type=F32)
     part[...] = value
     sent = [exchange(part, got_part.at[sp], part_s.at[p], part_r.at[sp], at_space(p)) for p in spaces]
+    p5_in.wait()
     for h in range(3):
         at = slice(h * channels // 3, (h + 1) * channels // 3)
         proj = lax.dot_general(places[at], p5_ref[...], ACROSS, preferred_element_type=F32)
@@ -329,6 +361,7 @@
     def landing(place):
         return s_pad.at[pl.ds(pl.multiple_of(place * cells, cells), cells)]
 
+    p4_in.wait()
     part_rows = images * cells // 2
     for h in range(2):
         at = slice(h * part_rows, (h + 1) * part_rows)
@@ -412,11 +445,36 @@
         return carry
 
     lax.fori_loop(0, tiles, tile, 0)
+    parts = ((0, GROUP // 2 - 1), (GROUP // 2 - 1, GROUP // 2))
+
+    def gathered(first, last):
+        for b in range(first, last):
+            pair = []
+            for slot in (2 * b, 2 * b + 1):
+                for p in spaces:
+                    arrived(
+                        sums.at[p, slot], got_space.at[p, slot], space_s.at[p, slot],
+                        space_r.at[p, slot], at_space(p),
+                    )
+                block = sums[sp, slot].astype(F32)
+                for p in spaces:
+                    block += got_space[p, slot].astype(F32)
+                pair.append(block.reshape(Y, 8, LANES))
+            send_y[:, b] = jnp.concatenate(pair, axis=1).astype(BF16)
+        h = parts.index((first, last))
+        for p in ys:
+            sent.append(
+                exchange(
+                    send_y.at[p, first:last], got_y.at[y, first:last], y_s.at[h, p], y_r.at[h, y], at_y(p)
+                )
+            )
+
+    gathered(*parts[0])
+    finish(tiles - 1)
+    send_block(GROUP - 1, GROUP - 1)
     back[...] = lax.dot_general(
         bpre[...], exp_ref[...], ACROSS, preferred_element_type=F32
     ).astype(BF16)
-    finish(tiles - 1)
-    send_block(GROUP - 1, GROUP - 1)
 
     rows = back.shape[0] // GROUP
 
@@ -430,44 +488,43 @@
     own = pltpu.make_async_copy(rows_of(sp), cots_ref.at[sp], local_sem)
     own.start()
 
-    for b in range(GROUP // 2):
-        pair = []
-        for slot in (2 * b, 2 * b + 1):
-            for p in spaces:
-                arrived(
-                    sums.at[p, slot], got_space.at[p, slot], space_s.at[p, slot],
-                    space_r.at[p, slot], at_space(p),
-                )
-            block = sums[sp, slot].astype(F32)
-            for p in spaces:
-                block += got_space[p, slot].astype(F32)
-            pair.append(block.reshape(Y, 8, LANES))
-        send_y[:, b] = jnp.concatenate(pair, axis=1).astype(BF16)
-
-    sent += [exchange(send_y.at[p], got_y.at[y], y_s.at[p], y_r.at[y], at_y(p)) for p in ys]
-    for p in ys:
-        arrived(send_y.at[p], got_y.at[p], y_s.at[p], y_r.at[p], at_y(p))
-    summed = send_y[y].astype(F32)
-    for p in ys:
-        summed += got_y[p].astype(F32)
-    own_z[...] = summed
-
-    sent += [exchange(own_z, got_z.at[z], z_s.at[p], z_r.at[z], at_z(p)) for p in zs]
-    for p in zs:
-        arrived(own_z, got_z.at[p], z_s.at[p], z_r.at[p], at_z(p))
-    for p in zs:
-        summed += got_z[p]
-    summed = (summed * scale).reshape(GROUP, 8, LANES)
-    kept = summed[:, :KEEP]
-    for p in range(1, Z):
-        kept = jnp.where(z == p, summed[:, KEEP * p : KEEP * (p + 1)], kept)
-    for b in range(GROUP):
-        pick[KEEP * b : KEEP * (b + 1)] = kept[b]
-
-    out_ref[sp] = pick[...]
-    sent += [exchange(pick, out_ref.at[sp], all_s.at[p], all_r.at[sp], at_space(p)) for p in spaces]
-    for p in spaces:
-        arrived(pick, out_ref.at[p], all_s.at[p], all_r.at[p], at_space(p))
+    gathered(GROUP // 2 - 1, GROUP // 2)
+    summed = []
+    for h, (first, last) in enumerate(parts):
+        for p in ys:
+            arrived(send_y.at[p, first:last], got_y.at[p, first:last], y_s.at[h, p], y_r.at[h, p], at_y(p))
+        value = send_y[y, first:last].astype(F32)
+        for p in ys:
+            value += got_y[p, first:last].astype(F32)
+        summed.append(value)
+    summed = (jnp.concatenate(summed, axis=0) * scale).reshape(GROUP, 8, LANES)
+
+    for p in range(Z):
+        for b in range(GROUP):
+            send_z[p, KEEP * b : KEEP * (b + 1)] = summed[b, KEEP * p : KEEP * (p + 1)]
+    me = z * 2 + z_lo
+    sent += [
+        exchange(send_z.at[p], got_z.at[me], z_s.at[p, e], z_r.at[me], at_line((p, e))) for p, e in line
+    ]
+    got_z[me] = send_z[z]
+    for p, e in line:
+        arrived(send_z.at[p], got_z.at[p * 2 + e], z_s.at[p, e], z_r.at[p * 2 + e], at_line((p, e)))
+    for e in range(GROUP // X):
+        value = got_z[e]
+        for p in range(1, Z):
+            value += got_z[p * 2 + e]
+        pick[e] = value
+
+    got_x[x] = pick[...]
+    sent += [exchange(pick, got_x.at[x], all_s.at[p], all_r.at[x], at_x(p)) for p in xs]
+    for p in xs:
+        arrived(pick, got_x.at[p], all_s.at[p], all_r.at[p], at_x(p))
+    for b in range(tiles * SEGS):
+        t, q = divmod(b, SEGS)
+        slot, owner = divmod(b, GROUP)
+        out_ref[KEEP * t : KEEP * (t + 1), q * LANES : (q + 1) * LANES] = got_x[
+            owner % X, owner // X, KEEP * slot : KEEP * (slot + 1)
+        ]
     for p in spaces:
         arrived(rows_of(p), cots_ref.at[p], cot_s.at[p], cot_r.at[p], at_space(p))
     own.wait()
@@ -508,6 +565,13 @@
     def _():
         for c in range(CHUNKS):
             up_copy(c).wait_send()
+
+
+def place_outputs(total, cots, grad_e, grad_d, grad_p, input_cotangent):
+    grad_p[...] = total[:, : grad_p.shape[1]]
+    grad_e[...] = total[:, 4 * LANES : 4 * LANES + grad_e.shape[1]]
+    grad_d[...] = total[:, 6 * LANES :][:, DW_AT : DW_AT + TAPS * TAPS]
+    input_cotangent[...] = cots[:, :, : input_cotangent.shape[3]].reshape(input_cotangent.shape)
 
 
 def local(
@@ -529,15 +593,21 @@
     vm = pl.BlockSpec(memory_space=pltpu.VMEM)
     dma = pltpu.SemaphoreType.DMA
     vmem = pltpu.VMEM
+    operands = (
+        expanded, dw_four, squeeze_down.T, squeeze_up, project_four.T, expand_five, dw_five, project_five.T,
+        cotangent.reshape(pixels, c5),
+    )
     total, cots = pl.pallas_call(
         functools.partial(kernel, 1.0 / math.sqrt(total_pixels)),
         out_shape=(
-            jax.ShapeDtypeStruct((GROUP, GROUP * KEEP, LANES), F32),
+            jax.ShapeDtypeStruct((tiles * KEEP, SEGS * LANES), F32),
             jax.ShapeDtypeStruct((GROUP, pixels // GROUP, wide4), BF16),
         ),
-        in_specs=[vm] * 9,
+        in_specs=[pl.BlockSpec(memory_space=pl.ANY)] * 9,
         out_specs=(vm, vm),
         scratch_shapes=[
+            *[vmem(a.shape, a.dtype) for a in operands],
+            dma((len(operands),)),
             vmem((images, W, channels), BF16),
             vmem((images, W, channels), BF16),
             vmem(expanded.shape, F32),
@@ -573,9 +643,10 @@
             vmem((GROUP, GROUP, half, LANES), BF16),
             vmem((Y, GROUP // 2, 16, LANES), BF16),
             vmem((Y, GROUP // 2, 16, LANES), BF16),
-            vmem((GROUP // 2, 16, LANES), F32),
-            vmem((Z, GROUP // 2, 16, LANES), F32),
-            vmem((GROUP * KEEP, LANES), F32),
+            vmem((Z, GROUP * KEEP, LANES), F32),
+            vmem((2 * Z, GROUP * KEEP, LANES), F32),
+            vmem((GROUP // X, GROUP * KEEP, LANES), F32),
+            vmem((X, GROUP // X, GROUP * KEEP, LANES), F32),
             dma((2, CHUNKS)),
             dma((2, CHUNKS)),
             dma((GROUP,)),
@@ -586,12 +657,12 @@
             dma((tiles,)),
             dma((GROUP, GROUP)),
             dma((GROUP, GROUP)),
-            dma((Y,)),
-            dma((Y,)),
-            dma((Z,)),
-            dma((Z,)),
-            dma((GROUP,)),
-            dma((GROUP,)),
+            dma((2, Y)),
+            dma((2, Y)),
+            dma((Z, 2)),
+            dma((2 * Z,)),
+            dma((X,)),
+            dma((X,)),
             dma((GROUP,)),
             dma((GROUP,)),
             dma(()),
@@ -602,19 +673,19 @@
         cost_estimate=pl.CostEstimate(
             flops=3_000_000_000, bytes_accessed=8_000_000, transcendentals=2_400_000
         ),
-    )(
-        expanded, dw_four, squeeze_down.T, squeeze_up, project_four.T, expand_five, dw_five, project_five.T,
-        cotangent.reshape(pixels, c5),
-    )
-    input_cotangent = cots[:, :, :c4].reshape(images, local_rows, W, c4)
-    total = total.reshape(GROUP, GROUP, KEEP, LANES).transpose(1, 0, 2, 3)
-    total = total.reshape(GROUP * GROUP, KEEP, LANES)[: tiles * SEGS]
-    total = total.reshape(tiles, SEGS, KEEP, LANES).transpose(0, 2, 1, 3)
-    total = total.reshape(tiles * KEEP, SEGS * LANES)
-    grad_p = total[:, :c5]
-    grad_e = total[:, 4 * LANES : 4 * LANES + c4].T
-    grad_d = total[:, 6 * LANES + DW_AT : 6 * LANES + DW_AT + TAPS * TAPS].T
-    return (grad_e, grad_d, grad_p, input_cotangent)
+    )(*operands)
+    grad_e, grad_d, grad_p, input_cotangent = pl.pallas_call(
+        place_outputs,
+        out_shape=(
+            jax.ShapeDtypeStruct((tiles * KEEP, c4), F32),
+            jax.ShapeDtypeStruct((tiles * KEEP, TAPS * TAPS), F32),
+            jax.ShapeDtypeStruct((tiles * KEEP, c5), F32),
+            jax.ShapeDtypeStruct((images, local_rows, W, c4), BF16),
+        ),
+        in_specs=[vm, vm],
+        out_specs=(vm, vm, vm, vm),
+    )(total, cots)
+    return (grad_e.T, grad_d.T, grad_p, input_cotangent)
 
 
 def solution(mesh):

time: 86.8 us -> 82.3 us (0.948)
  local copies, waits for them, and re-layouts: 3.67 us -> 0 us
  Pallas kernels: 82.3 us -> 81.3 us
    pallas_call x1, Pallas kernels: 82.3 us -> 79.5 us  [local(): pl.pallas_call(functools.partial(kernel, 1.0 / math.sqrt(total_pixels)),...]
    pallas_call x0 -> x1, Pallas kernels: none -> 1.84 us  [local(): pl.pallas_call(place_outputs, out_shape=(jax.ShapeDtypeStruct((tiles * KE...]
    transpose x3 -> x0, local copies, waits for them, and re-layouts: 1.3 us -> none  [the longest x1 0.67 us: local(): grad_d = total[:, 6 * LANES + DW_AT:6 * LANES + DW_AT + TAPS * TAPS].T]
    reshape x1 -> x0, local copies, waits for them, and re-layouts: 0.91 us -> none  [local(): total = total.reshape(GROUP, GROUP, KEEP, LANES).transpose(1, 0, 2, 3)]
where the time goes in v5:
time: 82.3 us; the launch traced here: 81.9 us
  Pallas kernels  81.3 us (99%)
    pallas_call x1, Pallas kernels, local(): pl.pallas_call(functools.partial(kernel, 1.0 / math.sqrt(total_pixels)),...  79.5 us
    pallas_call x1, Pallas kernels, local(): pl.pallas_call(place_outputs, out_shape=(jax.ShapeDtypeStruct((tiles * KE...  1.84 us

profile of v5, /device:TPU:6, one launch (start us, length us, event | category | flops | bytes accessed | tf_op | source)
XLA Modules:
  0.0 81.9 jit_solution(7537241632329390841)
XLA Ops:
  0.6 79.5 %shard_map.120 = (f32[18,896]{1,0:T(8,128)}, bf16[8,64,384]{2,1,0:T(8,128)(2,1)}) custom-call(bf16[8,4,16,1152]{3,2,1,0:T(8,128)(2,1)} %x_hbm.1, f32[9,1152]{1,0:T(8,128)} %dw4_hbm.1, bf16[86,1152]{1,0:T(8,128)(2,1)} %bitcast.9, bf16[86,1152]{1,0:T(8,128)(2,1)} %up_hbm.1, bf16[344,1152]{1,0:T(8,128)(2,1)} %bitcast.7, bf16[344,1152]{1,0:T(8,128)(2,1)} %e5_hbm.1, ...), custom_call_target="tpu_custom_call" | custom-call | flops 3000000000 | bytes 8000000 | tf_op jit(solution)/shard_map/pallas_call | solution.py:600
  80.1 1.8 %shard_map.121 = (f32[18,344]{1,0:T(8,128)}, f32[18,25]{1,0:T(8,128)}, f32[18,480]{1,0:T(8,128)}, bf16[8,4,16,344]{3,2,1,0:T(8,128)(2,1)}) custom-call(f32[18,896]{1,0:T(8,128)} %get-tuple-element.10.total, bf16[8,64,384]{2,1,0:T(8,128)(2,1)} %get-tuple-element.11.cots), custom_call_target="tpu_custom_call" | custom-call | tf_op jit(solution)/shard_map/pallas_call | solution.py:677

commit v6 on v5

--- a/solution.py
+++ b/solution.py
@@ -13,6 +13,7 @@
 Y, Z, CORES, KEEP = 8, 4, 2, 2
 GROUP = 8
 X = 4
+ORDER = (2, 6, 4, 1, 7, 3, 5, 0)
 CHUNKS = 4
 SEGS = 7
 DW_AT = 88
@@ -340,10 +341,14 @@
     part[...] = value
     sent = [exchange(part, got_part.at[sp], part_s.at[p], part_r.at[sp], at_space(p)) for p in spaces]
     p5_in.wait()
-    for h in range(3):
+
+    def reorder_project(h):
         at = slice(h * channels // 3, (h + 1) * channels // 3)
         proj = lax.dot_general(places[at], p5_ref[...], ACROSS, preferred_element_type=F32)
         proj_ref[at, : p5_ref.shape[0]] = proj.astype(BF16)
+
+    reorder_project(0)
+    reorder_project(1)
     for p in spaces:
         arrived(part, got_part.at[p], part_s.at[p], part_r.at[p], at_space(p))
     for p in spaces:
@@ -351,12 +356,13 @@
     squeezed = swish_rows(value).astype(BF16)
     gates[...] = sigmoid(jnp.dot(squeezed, up[...], preferred_element_type=F32))
 
-    for n in range(images):
-        gated = mixed[n].reshape(cells, channels) * gates[n : n + 1]
-        hid4[n * cells : (n + 1) * cells] = gated.astype(BF16)
-
-    def rows4_of(place):
-        return rows4.at[pl.ds(pl.multiple_of(place * cells, cells), cells)]
+    order = [lax.rem(sp + step, GROUP) for step in ORDER]
+    for k, n in enumerate(order):
+        gated = mixed[n].reshape(cells, channels) * gates[pl.ds(n, 1)]
+        hid4[k * cells : (k + 1) * cells] = gated.astype(BF16)
+
+    def rows4_of(k):
+        return rows4.at[k * cells : (k + 1) * cells]
 
     def landing(place):
         return s_pad.at[pl.ds(pl.multiple_of(place * cells, cells), cells)]
@@ -367,16 +373,14 @@
         at = slice(h * part_rows, (h + 1) * part_rows)
         value = lax.dot_general(hid4[at], p4_ref[...], ACROSS, preferred_element_type=F32)
         rows4[at, : p4_ref.shape[0]] = value.astype(BF16)
-        for n in range(h * images // 2, (h + 1) * images // 2):
-
-            @pl.when(sp != n)
-            def _():
-                exchange(
-                    rows4.at[n * cells : (n + 1) * cells], landing(sp), sec_s.at[n], sec_r.at[sp], at_space(n)
-                )
+        for k in range(h * images // 2, min((h + 1) * images // 2, images - 1)):
+            n = order[k]
+            exchange(rows4_of(k), landing(sp), sec_s.at[n], sec_r.at[sp], at_space(n))
 
     mine_at = pl.ds(pl.multiple_of(sp * cells, cells), cells)
-    s_pad[mine_at] = rows4[mine_at]
+    s_pad[mine_at] = rows4[(images - 1) * cells :]
+
+    reorder_project(2)
 
     def back_hidden(t, carry):
         lanes = pl.ds(pl.multiple_of(t * LANES, LANES), LANES)
@@ -388,7 +392,13 @@
 
     lax.fori_loop(0, tiles, back_hidden, 0)
     for p in spaces:
-        arrived(rows4_of(p), landing(p), sec_s.at[p], sec_r.at[p], at_space(p))
+        arrived(rows4_of(0), landing(p), sec_s.at[p], sec_r.at[p], at_space(p))
+
+    for h in range(3):
+        wide = channels // 3
+        value = jnp.dot(s_pad[...], exp_ref[:, h * wide : (h + 1) * wide], preferred_element_type=F32)
+        for t in range(tiles // 3):
+            pre[h * (tiles // 3) + t] = value[:, t * LANES : (t + 1) * LANES].reshape(H, W, LANES)
 
     def put(t, q, block):
         low, high = block[:half], block[half:]
@@ -405,7 +415,8 @@
 
     def finish(t):
         arrived(give.at[t], got_core.at[t], core_s.at[t], core_r.at[t], sibling)
-        for q in range(SEGS):
+        for step in range(SEGS):
+            q = lax.rem(sp + step, SEGS)
             b = t * SEGS + q
             owner, slot = lax.rem(b, GROUP), lax.div(b, GROUP)
             sums[owner, slot] = (mine[t, q] + got_core[t, q].astype(F32)).astype(BF16)
@@ -413,12 +424,8 @@
 
     def tile(t, carry):
         lanes = pl.ds(pl.multiple_of(t * LANES, LANES), LANES)
-        exp = exp_ref[:, lanes]
-        pre_v = jnp.dot(s_pad[...], exp, preferred_element_type=F32)
-        pre[...] = pre_v.reshape(H, W, LANES)
-        spread[2 : 2 + H] = (
-            (pre_v * sigmoid(pre_v)).astype(BF16).astype(F32).reshape(H, W, LANES)
-        )
+        pre_v = pre[t]
+        spread[2 : 2 + H] = (pre_v * sigmoid(pre_v)).astype(BF16).astype(F32)
         taps = [dw_ref[k : k + 1, lanes].reshape(1, 1, LANES) for k in range(TAPS * TAPS)]
         tile_forward(taps, spread, bhid.at[t], hid, bdeep)
         gp = lax.dot_general(
@@ -427,7 +434,7 @@
         )
         for q in range(4):
             put(t, q, gp[:, q * LANES : (q + 1) * LANES])
-        tile_backward(taps, spread, bdeep, pre, bpre.at[:, lanes], gtaps)
+        tile_backward(taps, spread, bdeep, pre.at[t], bpre.at[:, lanes], gtaps)
         bp = bpre[:, lanes]
         ge = lax.dot_general(
             bp, s_pad[...], (((0,), (0,)), ((), ())), preferred_element_type=F32
@@ -552,7 +559,7 @@
     lax.fori_loop(0, GROUP, drain_space, 0)
     for p in spaces:
         pltpu.make_async_remote_copy(
-            src_ref=rows4_of(p), dst_ref=landing(sp), send_sem=sec_s.at[p], recv_sem=sec_r.at[sp],
+            src_ref=rows4_of(0), dst_ref=landing(sp), send_sem=sec_s.at[p], recv_sem=sec_r.at[sp],
             device_id=at_space(p), device_id_type=MESH,
         ).wait_send()
 
@@ -627,7 +634,7 @@
             vmem((channels, wide5), BF16),
             vmem((pixels, wide4), BF16),
             vmem((pixels, wide5), BF16),
-            vmem((H, W, LANES), F32),
+            vmem((tiles, H, W, LANES), F32),
             vmem((H + 4, W, LANES), F32),
             vmem((tiles, H, W, LANES), F32),
             vmem((H, W, LANES), BF16),

time: 82.3 us -> 79.7 us (0.968)
  Pallas kernels: 81.3 us -> 78.7 us
    pallas_call x1, Pallas kernels: 79.5 us -> 76.9 us  [local(): pl.pallas_call(functools.partial(kernel, 1.0 / math.sqrt(total_pixels)),...]
where the time goes in v6:
time: 79.7 us; the launch traced here: 79.3 us
  Pallas kernels  78.7 us (99%)
    pallas_call x1, Pallas kernels, local(): pl.pallas_call(functools.partial(kernel, 1.0 / math.sqrt(total_pixels)),...  76.9 us
    pallas_call x1, Pallas kernels, local(): pl.pallas_call(place_outputs, out_shape=(jax.ShapeDtypeStruct((tiles * KE...  1.84 us

profile of v6, /device:TPU:6, one launch (start us, length us, event | category | flops | bytes accessed | tf_op | source)
XLA Modules:
  0.0 79.3 jit_solution(714316169405162757)
XLA Ops:
  0.6 76.9 %shard_map.120 = (f32[18,896]{1,0:T(8,128)}, bf16[8,64,384]{2,1,0:T(8,128)(2,1)}) custom-call(bf16[8,4,16,1152]{3,2,1,0:T(8,128)(2,1)} %x_hbm.1, f32[9,1152]{1,0:T(8,128)} %dw4_hbm.1, bf16[86,1152]{1,0:T(8,128)(2,1)} %bitcast.9, bf16[86,1152]{1,0:T(8,128)(2,1)} %up_hbm.1, bf16[344,1152]{1,0:T(8,128)(2,1)} %bitcast.7, bf16[344,1152]{1,0:T(8,128)(2,1)} %e5_hbm.1, ...), custom_call_target="tpu_custom_call" | custom-call | flops 3000000000 | bytes 8000000 | tf_op jit(solution)/shard_map/pallas_call | solution.py:607
  77.5 1.8 %shard_map.121 = (f32[18,344]{1,0:T(8,128)}, f32[18,25]{1,0:T(8,128)}, f32[18,480]{1,0:T(8,128)}, bf16[8,4,16,344]{3,2,1,0:T(8,128)(2,1)}) custom-call(f32[18,896]{1,0:T(8,128)} %get-tuple-element.10.total, bf16[8,64,384]{2,1,0:T(8,128)(2,1)} %get-tuple-element.11.cots), custom_call_target="tpu_custom_call" | custom-call | tf_op jit(solution)/shard_map/pallas_call | solution.py:684

commit v7 on v6

--- a/solution.py
+++ b/solution.py
@@ -357,10 +357,6 @@
     gates[...] = sigmoid(jnp.dot(squeezed, up[...], preferred_element_type=F32))
 
     order = [lax.rem(sp + step, GROUP) for step in ORDER]
-    for k, n in enumerate(order):
-        gated = mixed[n].reshape(cells, channels) * gates[pl.ds(n, 1)]
-        hid4[k * cells : (k + 1) * cells] = gated.astype(BF16)
-
     def rows4_of(k):
         return rows4.at[k * cells : (k + 1) * cells]
 
@@ -370,6 +366,10 @@
     p4_in.wait()
     part_rows = images * cells // 2
     for h in range(2):
+        for k in range(h * images // 2, (h + 1) * images // 2):
+            n = order[k]
+            gated = mixed[n].reshape(cells, channels) * gates[pl.ds(n, 1)]
+            hid4[k * cells : (k + 1) * cells] = gated.astype(BF16)
         at = slice(h * part_rows, (h + 1) * part_rows)
         value = lax.dot_general(hid4[at], p4_ref[...], ACROSS, preferred_element_type=F32)
         rows4[at, : p4_ref.shape[0]] = value.astype(BF16)
@@ -488,6 +488,7 @@
     def rows_of(place):
         return back.at[pl.ds(pl.multiple_of(place * rows, rows), rows)]
 
+    gathered(GROUP // 2 - 1, GROUP // 2)
     sent += [
         exchange(rows_of(p), cots_ref.at[sp], cot_s.at[p], cot_r.at[sp], at_space(p))
         for p in spaces
@@ -495,7 +496,6 @@
     own = pltpu.make_async_copy(rows_of(sp), cots_ref.at[sp], local_sem)
     own.start()
 
-    gathered(GROUP // 2 - 1, GROUP // 2)
     summed = []
     for h, (first, last) in enumerate(parts):
         for p in ys:

time: 79.7 us -> 78.9 us (0.990)
  Pallas kernels: 78.7 us -> 77.9 us
where the time goes in v7:
time: 78.9 us; the launch traced here: 78.6 us
  Pallas kernels  77.9 us (99%)
    pallas_call x1, Pallas kernels, local(): pl.pallas_call(functools.partial(kernel, 1.0 / math.sqrt(total_pixels)),...  76.1 us
    pallas_call x1, Pallas kernels, local(): pl.pallas_call(place_outputs, out_shape=(jax.ShapeDtypeStruct((tiles * KE...  1.84 us

profile of v7, /device:TPU:6, one launch (start us, length us, event | category | flops | bytes accessed | tf_op | source)
XLA Modules:
  0.0 78.6 jit_solution(17035970559741966380)
XLA Ops:
  0.6 76.1 %shard_map.120 = (f32[18,896]{1,0:T(8,128)}, bf16[8,64,384]{2,1,0:T(8,128)(2,1)}) custom-call(bf16[8,4,16,1152]{3,2,1,0:T(8,128)(2,1)} %x_hbm.1, f32[9,1152]{1,0:T(8,128)} %dw4_hbm.1, bf16[86,1152]{1,0:T(8,128)(2,1)} %bitcast.9, bf16[86,1152]{1,0:T(8,128)(2,1)} %up_hbm.1, bf16[344,1152]{1,0:T(8,128)(2,1)} %bitcast.7, bf16[344,1152]{1,0:T(8,128)(2,1)} %e5_hbm.1, ...), custom_call_target="tpu_custom_call" | custom-call | flops 3000000000 | bytes 8000000 | tf_op jit(solution)/shard_map/pallas_call | solution.py:607
  76.7 1.8 %shard_map.121 = (f32[18,344]{1,0:T(8,128)}, f32[18,25]{1,0:T(8,128)}, f32[18,480]{1,0:T(8,128)}, bf16[8,4,16,344]{3,2,1,0:T(8,128)(2,1)}) custom-call(f32[18,896]{1,0:T(8,128)} %get-tuple-element.10.total, bf16[8,64,384]{2,1,0:T(8,128)(2,1)} %get-tuple-element.11.cots), custom_call_target="tpu_custom_call" | custom-call | tf_op jit(solution)/shard_map/pallas_call | solution.py:684
